TPU v7x, 32 devices: a whole 2x2x4 slice. The times are simulated.
32 devices in a mesh: stream: 2 (over x), batch: 16 (over z, y, core).
Axes of the slice: x: 2, y: 2, z: 4, core: 2. Of those that a mesh axis runs over, the one named last changes fastest.
Arguments:
- inputs: float32 [16, 2, 768, 768], P('batch', 'stream'), may hold values from -12 to 12
- text_pages: int32 [16, 768], P('batch'), may hold values from 0 to 3, as said below
- text_boxes: int32 [16, 2, 768], P('batch'), may hold values from 0 to 15
- norm_gains: float32 [2, 2, 768], P('stream'), may hold values from 0.1 to 1.9
- norm_shifts: float32 [2, 2, 768], P('stream'), may hold values from -1.8 to 1.8
- w_query: bfloat16 [2, 768, 768], P('stream'), may hold values from -0.21875 to 0.21875
- w_key: bfloat16 [2, 768, 768], P('stream'), may hold values from -0.21875 to 0.21875
- w_value: bfloat16 [2, 768, 768], P('stream'), may hold values from -0.21875 to 0.21875
- w_out: bfloat16 [2, 768, 768], P('stream'), may hold values from -1.75 to 1.75
- w_up: bfloat16 [2, 768, 3072], P('stream'), may hold values from -0.21875 to 0.21875
- up_bias: float32 [2, 3072], P('stream'), may hold values from -1.8 to 1.8
- w_down: bfloat16 [2, 3072, 768], P('stream'), may hold values from -0.109375 to 0.109375
- down_bias: float32 [2, 768], P('stream'), may hold values from -1.8 to 1.8
- box_table: float32 [2, 14, 12], P('stream'), may hold values from -4 to 4
- cotangent: float32 [16, 2, 768, 768], P('batch', 'stream'), may hold values from -6 to 6
Outputs:
- block_out: float32 [16, 2, 768, 768], P('batch', 'stream')
- grad_inputs: float32 [16, 2, 768, 768], P('batch', 'stream')
- grad_norm_gains: float32 [2, 2, 768], P('stream')
- grad_norm_shifts: float32 [2, 2, 768], P('stream')
- grad_w_query: float32 [2, 768, 768], P('stream', 'batch')
- grad_w_key: float32 [2, 768, 768], P('stream', 'batch')
- grad_w_value: float32 [2, 768, 768], P('stream', 'batch')
- grad_w_out: float32 [2, 768, 768], P('stream', 'batch')
- grad_w_up: float32 [2, 768, 3072], P('stream', 'batch')
- grad_up_bias: float32 [2, 3072], P('stream')
- grad_w_down: float32 [2, 3072, 768], P('stream', 'batch')
- grad_down_bias: float32 [2, 768], P('stream')
- grad_box_table: float32 [2, 14, 12], P('stream')
- stats: float32 [2], replicated
Inputs may be any that keep to these rules, and one draw needn't show every extreme that they name: `text_pages`: each row's text slots hold pages 0, 1, ..., 2 in order, each page non-empty, followed by padding slots marked 3; a row holds 384 to 768 text tokens, and both ends occur.
All inputs are finite; a program needn't handle non-finite values.
Results may differ from a plain program's by a relative error of at most 0.012.
Values may be sent and summed in bfloat16 or wider, within the bound.
A program may use at most 320 MiB of HBM per device.

v0:
```python
import jax
import jax.numpy as jnp
from jax import lax
from jax.sharding import PartitionSpec as P

GRID = 16
PAGES = 3


masked_fill = -1e30


def partner(block, axis, bit):
    count = lax.axis_size(axis)
    route = []
    for low in range(count):
        high = low | 1 << bit
        if high != low and high < count:
            route += [(low, high), (high, low)]
    return lax.ppermute(block, axis, route)


def norm_forward(values, gain_row, shift_row):
    center = values - jnp.mean(values, axis=-1, keepdims=True)
    inverse = lax.rsqrt(jnp.mean(center * center, axis=-1, keepdims=True) + 1e-05)
    normal_part = center * inverse
    return (normal_part * gain_row + shift_row, normal_part, inverse)


def norm_backward(grad_normed, normal_part, inverse, gain_row):
    scaled = grad_normed * gain_row
    first_mean = jnp.mean(scaled, axis=-1, keepdims=True)
    second_mean = jnp.mean(scaled * normal_part, axis=-1, keepdims=True)
    return inverse * (scaled - first_mean - normal_part * second_mean)


def bucket_offset(own_coord, far_coord, bucket_count):
    radius = (bucket_count - 1) // 2
    return jnp.clip(own_coord[:, None] - far_coord[None, :], -radius, radius) + radius


def bias_from(rel_table, offset):
    result = jnp.zeros((rel_table.shape[1],) + offset.shape, jnp.float32)
    for bucket in range(rel_table.shape[0]):
        result = (
            result + rel_table[bucket][:, None, None] * (offset == bucket).astype(jnp.float32)[None]
        )
    return result


def bias_grad(grad_wide, offset, bucket_count):
    return jnp.stack(
        [
            jnp.sum(grad_wide * (offset == bucket).astype(jnp.float32)[None], axis=(1, 2))
            for bucket in range(bucket_count)
        ]
    )


def project(left, right):
    return jnp.einsum("rsd,de->rse", left, right, preferred_element_type=jnp.float32)


def weight_grad(left, right):
    return jnp.einsum("rsd,rse->de", left, right, preferred_element_type=jnp.float32)


def back_project(grad_low, weight):
    return jnp.einsum("rse,de->rsd", grad_low, weight, preferred_element_type=jnp.float32)


def on_device(
    inputs,
    text_pages,
    text_boxes,
    norm_gains,
    norm_shifts,
    w_query,
    w_key,
    w_value,
    w_out,
    w_up,
    up_bias,
    w_down,
    down_bias,
    box_table,
    cotangent,
):
    slot_count = inputs.shape[2]
    model_width = inputs.shape[3]
    head_count = box_table.shape[2]
    head_size = model_width // head_count
    bucket_count = box_table.shape[1] // 2
    score_scale = head_size ** (-0.5)
    is_text = lax.axis_index("stream") == 0
    positions = jnp.arange(slot_count, dtype=jnp.int32)
    cell_index = positions % (GRID * GRID)
    vision_page = positions // (GRID * GRID)
    vision_first = cell_index % GRID
    vision_second = cell_index // GRID
    own_valid = jnp.where(is_text, text_pages < PAGES, True).astype(jnp.float32)
    gain_rows = norm_gains[0]
    shift_rows = norm_shifts[0]
    rel_table = box_table[0]
    block_in = inputs[:, 0]
    normed_one, plain_one, inverse_one = norm_forward(block_in, gain_rows[0], shift_rows[0])
    normed_low = normed_one.astype(jnp.bfloat16)
    query = project(normed_low, w_query[0]).astype(jnp.bfloat16)
    own_keys = project(normed_low, w_key[0]).astype(jnp.bfloat16)
    own_values = project(normed_low, w_value[0]).astype(jnp.bfloat16)
    far_keys, far_values = partner((own_keys, own_values), "stream", 0)

    def geometry(row_index):
        text_page = text_pages[row_index]
        own_page = jnp.where(is_text, text_page, vision_page)
        far_page = jnp.where(is_text, vision_page, text_page)
        own_first = jnp.where(is_text, text_boxes[row_index, 0], vision_first)
        far_first = jnp.where(is_text, vision_first, text_boxes[row_index, 0])
        own_second = jnp.where(is_text, text_boxes[row_index, 1], vision_second)
        far_second = jnp.where(is_text, vision_second, text_boxes[row_index, 1])
        allowed = (own_page[:, None] == far_page[None, :]) | (own_page[:, None] == PAGES)
        return (
            allowed,
            bucket_offset(own_first, far_first, bucket_count),
            bucket_offset(own_second, far_second, bucket_count),
        )

    def heads_of(matrix):
        return matrix.reshape(slot_count, head_count, head_size)

    def score_block(row_index, allowed, offset_first, offset_second):
        raw = (
            jnp.einsum(
                "ihd,jhd->hij",
                heads_of(query[row_index]),
                heads_of(far_keys[row_index]),
                preferred_element_type=jnp.float32,
            )
            * score_scale
        )
        raw = (
            raw
            + bias_from(rel_table[:bucket_count], offset_first)
            + bias_from(rel_table[bucket_count:], offset_second)
        )
        return jnp.where(allowed[None], raw, masked_fill)

    row_index = 0
    allowed, offset_first, offset_second = geometry(row_index)
    masked = score_block(row_index, allowed, offset_first, offset_second)
    top_score = jnp.max(masked, axis=-1, keepdims=True)
    exp_scores = jnp.exp(masked - top_score)
    row_total = jnp.sum(exp_scores, axis=-1, keepdims=True)
    prob_low = (exp_scores / row_total).astype(jnp.bfloat16)
    attended = jnp.einsum(
        "hij,jhd->ihd",
        prob_low,
        heads_of(far_values[row_index]),
        preferred_element_type=jnp.float32,
    ).reshape(slot_count, model_width)
    attended_rows = [(attended * own_valid[row_index][:, None]).astype(jnp.bfloat16)]
    log_totals = [top_score + jnp.log(row_total)]
    attended_low = jnp.stack(attended_rows)
    branch_one = project(attended_low, w_out[0])
    middle = block_in + branch_one
    normed_two, plain_two, inverse_two = norm_forward(middle, gain_rows[1], shift_rows[1])
    normed_two_low = normed_two.astype(jnp.bfloat16)
    pre_act = project(normed_two_low, w_up[0]) + up_bias[0]
    act_low = jax.nn.gelu(pre_act).astype(jnp.bfloat16)
    branch_two = project(act_low, w_down[0]) + down_bias[0]
    block_out = middle + branch_two
    sublayer = branch_one + branch_two
    totals = lax.psum(
        (
            jnp.sum(own_valid * jnp.sum(block_out * block_out, axis=-1)),
            jnp.sum(own_valid * jnp.sum(sublayer * sublayer, axis=-1)),
            jnp.sum(own_valid),
        ),
        ("stream", "batch"),
    )
    denominator = totals[2] * model_width
    stats = jnp.stack([jnp.sqrt(totals[0] / denominator), jnp.sqrt(totals[1] / denominator)])
    grad_out = cotangent[:, 0]
    grad_out_low = grad_out.astype(jnp.bfloat16)
    grad_w_down = weight_grad(act_low, grad_out_low)
    grad_down_bias = jnp.sum(grad_out_low.astype(jnp.float32), axis=(0, 1))
    grad_act = back_project(grad_out_low, w_down[0])
    gelu_back = jax.vjp(jax.nn.gelu, pre_act)[1]
    grad_pre_low = gelu_back(grad_act)[0].astype(jnp.bfloat16)
    grad_w_up = weight_grad(normed_two_low, grad_pre_low)
    grad_up_bias = jnp.sum(grad_pre_low.astype(jnp.float32), axis=(0, 1))
    grad_normed_two = back_project(grad_pre_low, w_up[0])
    grad_gain_two = jnp.sum(grad_normed_two * plain_two, axis=(0, 1))
    grad_shift_two = jnp.sum(grad_normed_two, axis=(0, 1))
    grad_middle = grad_out + norm_backward(grad_normed_two, plain_two, inverse_two, gain_rows[1])
    grad_middle_low = grad_middle.astype(jnp.bfloat16)
    grad_w_out = weight_grad(attended_low, grad_middle_low)
    grad_attended = back_project(grad_middle_low, w_out[0]).astype(jnp.bfloat16) * own_valid[
        :, :, None
    ].astype(jnp.bfloat16)
    query_grad_rows, key_grad_rows, value_grad_rows = ([], [], [])
    row_index = 0
    allowed, offset_first, offset_second = geometry(row_index)
    masked = score_block(row_index, allowed, offset_first, offset_second)
    prob = jnp.exp(masked - log_totals[row_index])
    grad_heads = heads_of(grad_attended[row_index])
    grad_prob = jnp.einsum(
        "ihd,jhd->hij",
        grad_heads,
        heads_of(far_values[row_index]),
        preferred_element_type=jnp.float32,
    )
    inner_sum = jnp.sum(prob * grad_prob, axis=-1, keepdims=True)
    grad_score_low = (prob * (grad_prob - inner_sum)).astype(jnp.bfloat16)
    grad_score_wide = grad_score_low.astype(jnp.float32)
    grad_table = jnp.concatenate(
        [
            bias_grad(grad_score_wide, offset_first, bucket_count),
            bias_grad(grad_score_wide, offset_second, bucket_count),
        ],
        axis=0,
    )
    query_grad = (
        jnp.einsum(
            "hij,jhd->ihd",
            grad_score_low,
            heads_of(far_keys[row_index]),
            preferred_element_type=jnp.float32,
        )
        * score_scale
    )
    key_grad = (
        jnp.einsum(
            "hij,ihd->jhd",
            grad_score_low,
            heads_of(query[row_index]),
            preferred_element_type=jnp.float32,
        )
        * score_scale
    )
    value_grad = jnp.einsum(
        "hij,ihd->jhd", prob.astype(jnp.bfloat16), grad_heads, preferred_element_type=jnp.float32
    )
    query_grad_rows.append(query_grad.reshape(slot_count, model_width).astype(jnp.bfloat16))
    key_grad_rows.append(key_grad.reshape(slot_count, model_width).astype(jnp.bfloat16))
    value_grad_rows.append(value_grad.reshape(slot_count, model_width).astype(jnp.bfloat16))
    grad_query_low = jnp.stack(query_grad_rows)
    own_key_grad, own_value_grad = partner(
        (jnp.stack(key_grad_rows), jnp.stack(value_grad_rows)), "stream", 0
    )
    grad_w_query = weight_grad(normed_low, grad_query_low)
    grad_w_key = weight_grad(normed_low, own_key_grad)
    grad_w_value = weight_grad(normed_low, own_value_grad)
    grad_normed_one = (
        back_project(grad_query_low, w_query[0])
        + back_project(own_key_grad, w_key[0])
        + back_project(own_value_grad, w_value[0])
    )
    grad_gain_one = jnp.sum(grad_normed_one * plain_one, axis=(0, 1))
    grad_shift_one = jnp.sum(grad_normed_one, axis=(0, 1))
    grad_inputs = grad_middle + norm_backward(grad_normed_one, plain_one, inverse_one, gain_rows[0])
    big_sums = (
        lax.psum_scatter(grad_w_query, "batch", scatter_dimension=0, tiled=True),
        lax.psum_scatter(grad_w_key, "batch", scatter_dimension=0, tiled=True),
        lax.psum_scatter(grad_w_value, "batch", scatter_dimension=0, tiled=True),
        lax.psum_scatter(grad_w_out, "batch", scatter_dimension=0, tiled=True),
        lax.psum_scatter(grad_w_up, "batch", scatter_dimension=0, tiled=True),
        lax.psum_scatter(grad_w_down, "batch", scatter_dimension=0, tiled=True),
    )
    small_sums = lax.psum(
        (
            jnp.stack([grad_gain_one, grad_gain_two]),
            jnp.stack([grad_shift_one, grad_shift_two]),
            grad_up_bias,
            grad_down_bias,
            grad_table,
        ),
        "batch",
    )
    return (
        block_out[:, None],
        grad_inputs[:, None],
        small_sums[0][None],
        small_sums[1][None],
        big_sums[0][None],
        big_sums[1][None],
        big_sums[2][None],
        big_sums[3][None],
        big_sums[4][None],
        small_sums[2][None],
        big_sums[5][None],
        small_sums[3][None],
        small_sums[4][None],
        stats,
    )


def solution(mesh):
    placed = (
        P("batch", "stream", None, None),
        P("batch", None),
        P("batch", None, None),
        P("stream", None, None),
        P("stream", None, None),
        P("stream", None, None),
        P("stream", None, None),
        P("stream", None, None),
        P("stream", None, None),
        P("stream", None, None),
        P("stream", None),
        P("stream", None, None),
        P("stream", None),
        P("stream", None, None),
        P("batch", "stream", None, None),
    )
    return jax.shard_map(
        on_device,
        mesh=mesh,
        in_specs=placed,
        out_specs=(
            P("batch", "stream", None, None),
            P("batch", "stream", None, None),
            P("stream", None, None),
            P("stream", None, None),
            P("stream", "batch", None),
            P("stream", "batch", None),
            P("stream", "batch", None),
            P("stream", "batch", None),
            P("stream", "batch", None),
            P("stream", None),
            P("stream", "batch", None),
            P("stream", None),
            P("stream", None, None),
            P(),
        ),
        check_vma=False,
    )
```

profile of v0, /device:TPU:0, one launch (start us, length us, event | category | flops | bytes accessed | tf_op | source)
XLA Modules:
  0.0 717.0 jit_solution(5941767930912588233)
XLA Ops:
  7.2 2.0 reduce_sum.319
  11.3 2.1 fusion.72
  13.5 2.9 collective-permute-start
  16.4 2.1 fusion.73
  19.8 2.1 copy.47
  26.9 3.9 convolution_convert_fusion.2
  30.9 2.0 copy.51
  34.2 2.0 compare_or_fusion
  36.1 6.6 fusion.52
  42.7 7.2 fusion.59
  49.9 18.1 %collective-permute-done.1 = bf16[1,768,768]{2,1,0:T(8,128)(2,1)} collective-permute-done((bf16[1,768,768]{2,1,0:T(8,128)(2,1)}, bf16[1,768,768]{2,1,0:T(8,128)(2,1)}, u32[]{:S(2)}, u32[]{:S(2)}) %collective-permute-start.1) | collective-permute-done | bytes 1179680 | tf_op jit(solution)/shard_map/ppermute | solution.py:20
  68.0 2.4 copy.49
  70.4 44.4 %fusion.121 = (f32[12,768]{1,0:T(8,128)}, f32[12,768,768]{1,2,0:T(8,128)}) fusion(f32[768,768]{0,1:T(8,128)} %get-tuple-element.115, f32[12]{0:T(128)} %get-tuple-element.84, f32[768,768]{0,1:T(8,128)} %get-tuple-element.116, f32[12]{0:T(128)} %get-tuple-element.85, f32[768,768]{0,1:T(8,128)} %get-tuple-element.117, f32[12]{0:T(128)S(1)} %copy-done.60, ...), kind=kOutput, calls=%fused_computation.221 | convolution fusion | flops 1125374976 | bytes 64328352 | tf_op jit(solution)/shard_map/ihd,jhd->hij/dot_general | solution.py:133
  114.8 12.9 %fusion.14 = f32[12,768]{1,0:T(8,128)S(1)} fusion(f32[12,768,768]{1,2,0:T(8,128)} %get-tuple-element.126, f32[12,768]{1,0:T(8,128)} %get-tuple-element.125), kind=kLoop, calls=%fused_computation.34 | loop fusion | flops 14146560 | bytes 28385280 | tf_op jit(solution)/shard_map/reduce_sum | solution.py:153
  128.3 1.6 copy.48
  129.9 11.8 %multiply_convert_fusion.4 = bf16[12,64,768]{2,1,0:T(8,128)(2,1)S(1)} fusion(bf16[768,12,64]{0,2,1:T(8,128)(2,1)S(1)} %bitcast.166, f32[12,768,768]{1,2,0:T(8,128)} %get-tuple-element.126, f32[12,768]{1,0:T(8,128)S(1)} %fusion.14, f32[12,768]{1,0:T(8,128)S(1)} %copy-done.27, f32[768]{0:T(1024)S(1)} %copy-done.37), kind=kOutput, calls=%fused_computation.78 | convolution fusion | flops 928382976 | bytes 30747648 | tf_op jit(solution)/shard_map/hij,jhd->ihd/dot_general | solution.py:155
  141.8 2.8 fusion.119
  145.4 4.2 fusion.33
  149.6 15.1 %convert_reduce_fusion = (f32[3072]{0:T(1024)}, bf16[768,3072]{1,0:T(8,128)(2,1)}) fusion(f32[768,3072]{1,0:T(8,128)S(1)} %fusion.33, f32[3072]{0:T(1024)S(1)} %bitcast.198, bf16[1,3072,768]{2,1,0:T(8,128)(2,1)} %param.26, f32[1,1,768,768]{3,2,1,0:T(8,128)S(1)} %copy-done.8), kind=kOutput, calls=%fused_computation.48 | convolution fusion | flops 3678729216 | bytes 21258240 | tf_op jit(solution)/shard_map/rse,de->rsd/dot_general | solution.py:69
  164.7 8.2 %fusion.122 = (f32[768]{0:T(1024)}, f32[768,768]{1,0:T(8,128)}) fusion(bf16[768,3072]{1,0:T(8,128)(2,1)} %get-tuple-element.134, bf16[1,768,3072]{2,1,0:T(8,128)(2,1)S(1)} %bitcast.161), kind=kOutput, calls=%fused_computation.222 | convolution fusion | flops 3624467712 | bytes 11799552 | tf_op jit(solution)/shard_map/rse,de->rsd/dot_general | solution.py:69
  172.9 3.2 copy.52
  176.1 13.6 %multiply_reduce_fusion.2 = (f32[768]{0:T(1024)}, f32[768]{0:T(1024)}, f32[768]{0:T(1024)S(1)}, f32[768]{0:T(1024)S(1)}, f32[768]{0:T(1024)}, /*index=5*/f32[1,1,768,768]{2,3,1,0:T(8,128)}) fusion(f32[768,768]{0,1:T(8,128)S(1)} %get-tuple-element.103, f32[768]{0:T(1024)} %reduce.53, f32[768,768]{0,1:T(8,128)} %get-tuple-element.127, f32[768,768]{0,1:T(8,128)} %copy.52, ...), kind=kOutput, calls=%fused_computation.66 | convolution fusion | flops 3656315136 | bytes 23632896 | tf_op jit(solution)/shard_map/rsd,de->rse/dot_general | solution.py:61
  190.5 1.4 copy-done.4
  192.0 2.6 fusion.95
  194.6 3.8 fusion.71
  198.4 22.8 %multiply_reduce_fusion = (f32[12,768]{1,0:T(8,128)}, f32[12,768,768]{1,2,0:T(8,128)}) fusion(f32[12,768,768]{1,2,0:T(8,128)} %get-tuple-element.126, f32[12,768]{1,0:T(8,128)} %log_add_fusion, bf16[768,12,64]{0,2,1:T(8,128)(2,1)} %bitcast.164, bf16[768,12,64]{0,2,1:T(8,128)(2,1)} %bitcast.167), kind=kOutput, calls=%fused_computation.29 | convolution fusion | flops 927194112 | bytes 59056128 | tf_op jit(solution)/shard_map/ihd,jhd->hij/dot_general | solution.py:207
  221.2 48.0 %fusion.13 = (f32[12]{0:T(128)}, f32[12]{0:T(128)}, f32[12]{0:T(128)}, f32[12]{0:T(128)}, f32[12]{0:T(128)}, /*index=5*/f32[12]{0:T(128)}, f32[12]{0:T(128)}, f3...) fusion(f32[768,768]{0,1:T(8,128)} %get-tuple-element.115, ...), kind=kLoop, calls=%fused_computation.27 | loop fusion | flops 233570096 | bytes 103883424 | tf_op jit(solution)/shard_map/reduce_sum | solution.py:54
  269.2 8.0 %multiply_convert_fusion.3 = bf16[12,64,768]{2,1,0:T(8,128)(2,1)S(1)} fusion(bf16[768,12,64]{0,2,1:T(8,128)(2,1)} %bitcast.159, bf16[12,768,768]{1,2,0:T(8,128)(2,1)} %get-tuple-element.101), kind=kOutput, calls=%fused_computation.74 | convolution fusion | flops 907149312 | bytes 16515072 | tf_op jit(solution)/shard_map/hij,jhd->ihd/dot_general | solution.py:224
  278.3 2.7 fusion.125
  281.1 12.5 %fusion.68 = bf16[12,64,768]{2,1,0:T(8,128)(2,1)S(1)} fusion(bf16[768,12,64]{0,2,1:T(8,128)(2,1)} %bitcast.165, f32[12,768,768]{1,2,0:T(8,128)} %get-tuple-element.126, f32[12,768]{1,0:T(8,128)} %log_add_fusion), kind=kOutput, calls=%fused_computation.119 | convolution fusion | flops 920715264 | bytes 30707712 | tf_op jit(solution)/shard_map/hij,ihd->jhd/dot_general | solution.py:241
  293.6 1.8 collective-permute-start.3
  295.4 25.2 %collective-permute-done.3 = bf16[1,768,768]{1,2,0:T(8,128)(2,1)S(1)} collective-permute-done((bf16[1,768,768]{1,2,0:T(8,128)(2,1)S(1)}, bf16[1,768,768]{1,2,0:T(8,128)(2,1)S(1)}, u32[]{:S(2)}, u32[]{:S(2)}) %collective-permute-start.3) | collective-permute-done | bytes 1179680 | tf_op jit(solution)/shard_map/ppermute | solution.py:20
  321.6 2.5 fusion.75
  324.2 9.9 %multiply_convert_fusion.2 = bf16[12,64,768]{2,1,0:T(8,128)(2,1)S(1)} fusion(bf16[768,12,64]{0,2,1:T(8,128)(2,1)} %bitcast.171, bf16[12,768,768]{1,2,0:T(8,128)(2,1)} %get-tuple-element.101), kind=kOutput, calls=%fused_computation.73 | convolution fusion | flops 907149312 | bytes 16515072 | tf_op jit(solution)/shard_map/hij,ihd->jhd/dot_general | solution.py:233
  334.1 1.4 collective-permute-start.2
  335.6 24.7 %collective-permute-done.2 = bf16[1,768,768]{1,2,0:T(8,128)(2,1)S(1)} collective-permute-done((bf16[1,768,768]{1,2,0:T(8,128)(2,1)S(1)}, bf16[1,768,768]{1,2,0:T(8,128)(2,1)S(1)}, u32[]{:S(2)}, u32[]{:S(2)}) %collective-permute-start.2) | collective-permute-done | bytes 1179680 | tf_op jit(solution)/shard_map/ppermute | solution.py:20
  361.3 2.6 fusion.78
  364.1 14.3 %fusion.82 = f32[3072,768]{1,0:T(8,128)} fusion(f32[1,1,768,768]{3,2,1,0:T(8,128)} %param.29, f32[768,3072]{1,0:T(8,128)} %copy-done.10, f32[3072]{0:T(1024)} %bitcast.197), kind=kOutput, calls=%fused_computation.131 | convolution fusion | flops 3648061440 | bytes 21245952 | tf_op jit(solution)/shard_map/rsd,rse->de/dot_general | solution.py:65
  378.5 8.8 %fusion.118 = f32[768,3072]{1,0:T(8,128)} fusion(bf16[768,3072]{1,0:T(8,128)(2,1)} %get-tuple-element.134, f32[768,768]{0,1:T(8,128)S(1)} %get-tuple-element.103, f32[768]{0:T(1024)S(1)} %get-tuple-element.70, f32[768]{0:T(1024)S(1)} %get-tuple-element.136, f32[768]{0:T(1024)S(1)} %add_rsqrt_fusion, f32[768]{0:T(1024)S(1)} %broadcast_multiply_fusion.4), kind=kOutput, calls=%fused_computation.219 | convolution fusion | flops 3626827776 | bytes 16527360 | tf_op jit(solution)/shard_map/rsd,rse->de/dot_general | solution.py:65
  387.3 1.7 copy-done.9
  390.3 40.5 %all-reduce = (f32[]{:T(128)}, f32[]{:T(128)}, f32[]{:T(128)}) all-reduce(f32[]{:T(128)} %get-tuple-element.89, f32[]{:T(128)} %get-tuple-element.90, f32[]{:T(128)} %get-tuple-element.88), channel_id=1, replica_groups=mesh['stream'=2,'batch'=16] {'stream','batch'}, use_global_device_ids=true, to_apply=%region_49.50 | all-reduce | flops 3 | bytes 24 | tf_op jit(solution)/shard_map/psum | solution.py:173
  433.6 3.2 copy.60
  437.6 2.5 fusion.90
  442.4 2.0 multiply_reduce_fusion.4
  446.3 2.0 copy.61
  449.6 59.6 %all-reduce.1 = (f32[1,2,768]{2,1,0:T(2,128)}, f32[1,2,768]{2,1,0:T(2,128)}, f32[1,3072]{1,0:T(1,128)}, f32[1,768]{1,0:T(1,128)}, f32[1,14,12]{2,1,0:T(8,128)S(1)}) all-reduce(f32[1,2,768]{2,1,0:T(2,128)S(1)} %maximum_bitcast_fusion, f32[1,2,768]{2,1,0:T(2,128)S(1)} %maximum_bitcast_fusion.1, ...), channel_id=1, replica_groups=mesh['stream'=2,'batch'=16] {'batch'}, use_global_device_ids=true, to_apply=%region_13.14 | all-reduce | flops 7080 | bytes 56640 | tf_op jit(solution)/shard_map/psum | solution.py:270
  510.0 83.7 %reduce-scatter.17.cloned.1.call-done = f32[192,768]{1,0:T(8,128)} async-done(((f32[3072,768]{1,0:T(8,128)}), f32[192,768]{1,0:T(8,128)}) %reduce-scatter.17.cloned.1.call-update) | async-done | bytes 589840 | tf_op jit(solution)/shard_map/reduce_scatter | solution.py:268
  593.7 116.2 %reduce-scatter.15.cloned.1.call-done = f32[48,3072]{1,0:T(8,128)} async-done(((f32[768,3072]{1,0:T(8,128)}), f32[48,3072]{1,0:T(8,128)}) %reduce-scatter.15.cloned.1.call-update) | async-done | bytes 589840 | tf_op jit(solution)/shard_map/reduce_scatter | solution.py:267
  (189 shorter events, 24.3 us)
Async XLA Ops:
  7.2 134.6 %copy-start = (bf16[1,768,768]{2,1,0:T(8,128)(2,1)S(1)}, bf16[1,768,768]{2,1,0:T(8,128)(2,1)}, u32[]{:S(2)}) copy-start(bf16[1,768,768]{2,1,0:T(8,128)(2,1)} %param.23) | copy-start | bytes 3538948
  7.2 502.8 %reduce-scatter.13.cloned.1.call-start = ((), (), s32[]{:S(2)}) async-start(), calls=%async_computation.9 | async-start | bytes 2506752 | tf_op jit(solution)/shard_map/reduce_scatter | solution.py:266
  10.1 3.3 copy-start.32
  11.3 5.1 copy-start.23
  11.3 5.1 copy-start.61
  13.5 5.1 copy-start.34
  13.5 114.8 %collective-permute-start = (bf16[1,768,768]{2,1,0:T(8,128)(2,1)}, bf16[1,768,768]{2,1,0:T(8,128)(2,1)}, u32[]{:S(2)}, u32[]{:S(2)}) collective-permute-start(bf16[1,768,768]{2,1,0:T(8,128)(2,1)} %fusion.72), channel_id=1, source_target_pairs={{0,16},{16,0},{1,17},{17,1},{2,18},{18,2},{3,19},{19,3},{4,20},{20... | collective-permute-start | bytes 3538952 | tf_op jit(solution)/shard_map/ppermute | solution.py:20
  18.5 49.4 %collective-permute-start.1 = (bf16[1,768,768]{2,1,0:T(8,128)(2,1)}, bf16[1,768,768]{2,1,0:T(8,128)(2,1)}, u32[]{:S(2)}, u32[]{:S(2)}) collective-permute-start(bf16[1,768,768]{2,1,0:T(8,128)(2,1)} %fusion.73), channel_id=1, source_target_pairs={{0,16},{16,0},{1,17},{17,1},{2,18},{18,2},{3,19},{19,3},{4,20},{20... | collective-permute-start | bytes 3538952 | tf_op jit(solution)/shard_map/ppermute | solution.py:20
  19.8 3.4 copy-start.18
  26.9 3.9 copy-start.7
  30.9 3.3 copy-start.36
  42.7 27.6 %copy-start.6 = (f32[768,768]{0,1:T(8,128)}, f32[768,768]{0,1:T(8,128)S(1)}, u32[]{:S(2)}) copy-start(f32[768,768]{0,1:T(8,128)S(1)} %get-tuple-element.107) | copy-start | bytes 7077892
  49.9 20.5 %copy-start.59 = (f32[12]{0:T(128)S(1)}, f32[12]{0:T(128)}, u32[]{:S(2)}) copy-start(f32[12]{0:T(128)} %get-tuple-element.72) | copy-start | bytes 148
  49.9 20.5 %copy-start.60 = (f32[12]{0:T(128)S(1)}, f32[12]{0:T(128)}, u32[]{:S(2)}) copy-start(f32[12]{0:T(128)} %get-tuple-element.73) | copy-start | bytes 148
  114.7 12.9 %copy-start.27 = (f32[12,768]{1,0:T(8,128)S(1)}, f32[12,768]{1,0:T(8,128)}, u32[]{:S(2)}) copy-start(f32[12,768]{1,0:T(8,128)} %get-tuple-element.125) | copy-start | bytes 110596
  129.9 11.9 %copy-start.15 = (bf16[1,768,768]{1,2,0:T(8,128)(2,1)}, bf16[1,768,768]{1,2,0:T(8,128)(2,1)S(1)}, u32[]{:S(2)}) copy-start(bf16[1,768,768]{1,2,0:T(8,128)(2,1)S(1)} %copy.48) | copy-start | bytes 3538948
  129.9 11.9 %copy-start.2 = (f32[1,1,768,768]{2,3,1,0:T(8,128)S(1)}, f32[1,1,768,768]{2,3,1,0:T(8,128)}, u32[]{:S(2)}) copy-start(f32[1,1,768,768]{2,3,1,0:T(8,128)} %copy.47) | copy-start | bytes 7077892
  141.8 3.5 slice-start
  141.8 3.6 slice-start.1
  145.3 4.2 copy-start.8
  145.3 4.3 copy-start.65
  149.6 15.1 %copy-start.10 = (f32[768,3072]{1,0:T(8,128)}, f32[768,3072]{1,0:T(8,128)S(1)}, u32[]{:S(2)}) copy-start(f32[768,3072]{1,0:T(8,128)S(1)} %fusion.33) | copy-start | bytes 28311556
  176.1 13.7 %copy-start.11 = (f32[1,1,768,768]{2,3,1,0:T(8,128)S(1)}, f32[1,1,768,768]{2,3,1,0:T(8,128)}, u32[]{:S(2)}) copy-start(f32[1,1,768,768]{2,3,1,0:T(8,128)} %copy.51) | copy-start | bytes 7077892
  176.1 13.7 %copy-start.12 = (f32[768,768]{0,1:T(8,128)S(1)}, f32[768,768]{0,1:T(8,128)}, u32[]{:S(2)}) copy-start(f32[768,768]{0,1:T(8,128)} %copy.52) | copy-start | bytes 7077892
  198.4 311.6 %reduce-scatter.7.cloned.1.call-start = ((), (), s32[]{:S(2)}) async-start(), calls=%async_computation.6 | async-start | bytes 2506752 | tf_op jit(solution)/shard_map/reduce_scatter | solution.py:263
  269.2 9.1 %copy-start.24 = (bf16[768,768]{1,0:T(8,128)(2,1)S(1)}, bf16[768,768]{1,0:T(8,128)(2,1)}, u32[]{:S(2)}) copy-start(bf16[768,768]{1,0:T(8,128)(2,1)} %copy-done.23) | copy-start | bytes 3538948
  281.0 228.9 %reduce-scatter.11.cloned.1.call-start = ((), (), s32[]{:S(2)}) async-start(), calls=%async_computation.8 | async-start | bytes 2506752 | tf_op jit(solution)/shard_map/reduce_scatter | solution.py:265
  281.1 40.5 %copy-start.25 = (bf16[768,768]{1,0:T(8,128)(2,1)S(1)}, bf16[768,768]{1,0:T(8,128)(2,1)}, u32[]{:S(2)}) copy-start(bf16[768,768]{1,0:T(8,128)(2,1)} %copy-done.23) | copy-start | bytes 3538948
  293.6 27.0 %collective-permute-start.3 = (bf16[1,768,768]{1,2,0:T(8,128)(2,1)S(1)}, bf16[1,768,768]{1,2,0:T(8,128)(2,1)S(1)}, u32[]{:S(2)}, u32[]{:S(2)}) collective-permute-start(bf16[1,768,768]{1,2,0:T(8,128)(2,1)S(1)} %bitcast.172), channel_id=1, source_target_pairs={{0,16},{16,0},{1,17},{17,1},{2,18},{18,2},{3,19},{19,3},{4,20},{20... | collective-permute-start | bytes 3538952 | tf_op jit(solution)/shard_map/ppermute | solution.py:20
  324.1 185.8 %reduce-scatter.9.cloned.1.call-start = ((), (), s32[]{:S(2)}) async-start(), calls=%async_computation.7 | async-start | bytes 2506752 | tf_op jit(solution)/shard_map/reduce_scatter | solution.py:264
  324.2 37.1 %copy-start.26 = (bf16[768,768]{1,0:T(8,128)(2,1)S(1)}, bf16[768,768]{1,0:T(8,128)(2,1)}, u32[]{:S(2)}) copy-start(bf16[768,768]{1,0:T(8,128)(2,1)} %copy-done.23) | copy-start | bytes 3538948
  334.1 26.2 %collective-permute-start.2 = (bf16[1,768,768]{1,2,0:T(8,128)(2,1)S(1)}, bf16[1,768,768]{1,2,0:T(8,128)(2,1)S(1)}, u32[]{:S(2)}, u32[]{:S(2)}) collective-permute-start(bf16[1,768,768]{1,2,0:T(8,128)(2,1)S(1)} %bitcast.173), channel_id=1, source_target_pairs={{0,16},{16,0},{1,17},{17,1},{2,18},{18,2},{3,19},{19,3},{4,20},{20... | collective-permute-start | bytes 3538952 | tf_op jit(solution)/shard_map/ppermute | solution.py:20
  363.9 229.8 %reduce-scatter.17.cloned.1.call-start = ((), (), s32[]{:S(2)}) async-start(), calls=%async_computation.11 | async-start | bytes 10027008 | tf_op jit(solution)/shard_map/reduce_scatter | solution.py:268
  378.4 331.5 %reduce-scatter.15.cloned.1.call-start = ((), (), s32[]{:S(2)}) async-start(), calls=%async_computation.10 | async-start | bytes 10027008 | tf_op jit(solution)/shard_map/reduce_scatter | solution.py:267
  389.0 41.9 %copy-start.41 = (f32[768]{0:T(1024)S(1)}, f32[768]{0:T(1024)}, u32[]{:S(2)}) copy-start(f32[768]{0:T(1024)} %get-tuple-element.131) | copy-start | bytes 9220
  389.0 43.9 %copy-start.40 = (f32[768]{0:T(1024)S(1)}, f32[768]{0:T(1024)}, u32[]{:S(2)}) copy-start(f32[768]{0:T(1024)} %get-tuple-element.66) | copy-start | bytes 9220
  433.5 3.3 copy-start.48
  433.5 3.3 copy-start.49
  433.5 3.3 copy-start.50
  433.5 3.3 copy-start.51
  433.5 3.3 copy-start.52
  433.6 3.3 copy-start.53
  433.6 3.3 copy-start.54
  433.6 3.3 copy-start.55
  433.6 3.3 copy-start.56
  433.6 3.3 copy-start.57
  433.6 3.3 copy-start.58
  433.6 3.9 copy-start.17
  (30 other events, 58.2 us)
Sparse Core Ops, SparseCore 0:
  198.5 64.5 reduce-scatter.12
  281.2 64.5 reduce-scatter.6
  350.0 61.9 reduce-scatter.10
  416.7 62.0 reduce-scatter.8
  483.3 110.3 reduce-scatter.16
  598.8 111.0 reduce-scatter.14
where the time goes:
time: 721 us; the launch traced here: 717 us
  waiting for transfers between devices  268 us (37%)
  matrix products  204 us (28%)
  blocking collectives  100 us (14%)
  other arithmetic  89.7 us (12%)
  local copies, waits for them, and re-layouts  31.1 us (4%)
  between operations  17.1 us (2%)
    reduce_scatter x1, waiting for transfers between devices, on_device(): lax.psum_scatter(grad_w_up, 'batch', scatter_dimension=0, tiled=True)  116 us
    reduce_scatter x1, waiting for transfers between devices, on_device(): lax.psum_scatter(grad_w_down, 'batch', scatter_dimension=0, tiled=True)  83.7 us
    ppermute x4, waiting for transfers between devices, partner(): return lax.ppermute(block, axis, route)  68 us
    psum x1, blocking collectives, on_device(): lax.psum((jnp.stack([grad_gain_one, grad_gain_two]), jnp.stack([grad_shif...  59.6 us
    reduce_sum x1, other arithmetic, bias_grad(): jnp.sum(grad_wide * (offset == bucket).astype(jnp.float32)[None], axis=(1...  48 us
    dot_general x1, matrix products, score_block(): jnp.einsum('ihd,jhd->hij', heads_of(query[row_index]), heads_of(far_keys[...  44.4 us
    psum x1, blocking collectives, on_device(): lax.psum((jnp.sum(own_valid * jnp.sum(block_out * block_out, axis=-1)), j...  40.5 us
    dot_general x6, matrix products, weight_grad(): jnp.einsum('rsd,rse->de', left, right, preferred_element_type=jnp.float32)  33.5 us
  transfers between devices with their start and end apart: 10, of which 5 were waited for; matrix products, arithmetic and copies ran while one was open for 34% of the time, Pallas kernels for 0%

commit v1 on v0

--- a/solution.py
+++ b/solution.py
@@ -1,6 +1,8 @@
 import jax
 import jax.numpy as jnp
 from jax import lax
+from jax.experimental import pallas as pl
+from jax.experimental.pallas import tpu as pltpu
 from jax.sharding import PartitionSpec as P
 
 GRID = 16
@@ -67,6 +69,149 @@
 
 def back_project(grad_low, weight):
     return jnp.einsum("rse,de->rsd", grad_low, weight, preferred_element_type=jnp.float32)
+
+
+MESH = pl.DeviceIdType.MESH
+
+
+def scatter_kernel(gd, gr, od, orr, cd, cr, yd, yr, zd, zr, ld, lr, csem, crem, ysem, yrem, zsem, zrem, lsem):
+    st = lax.axis_index("stream")
+    me = lax.axis_index("batch")
+    c = lax.rem(me, 2)
+    y = lax.rem(lax.div(me, 2), 2)
+    z = lax.div(me, 4)
+    core_peer = me + 1 - 2 * c
+    y_peer = me + 2 - 4 * y
+    z_peers = [lax.rem(z + k, 4) * 4 + y * 2 + c for k in (1, 2, 3)]
+    barrier = pltpu.get_barrier_semaphore()
+    for peer in [core_peer, y_peer] + z_peers:
+        pl.semaphore_signal(barrier, inc=1, device_id=(st, peer), device_id_type=MESH)
+    pl.semaphore_wait(barrier, 5)
+    wide, low = jnp.float32, jnp.bfloat16
+
+    def remote(source, target, send, recv, peer):
+        return pltpu.make_async_remote_copy(
+            source, target, send, recv, device_id=(st, peer), device_id_type=MESH
+        )
+
+    def chunk(p):
+        return lax.rem(z + p + 1, 4)
+
+    def core_copy(p):
+        if p < 4:
+            return remote(gd.at[chunk(p), :, 1 - c], cd.at[p], csem.at[p], crem.at[p], core_peer)
+        return remote(gr.at[p - 4, :, :, 1 - c], cr.at[p - 4], csem.at[p], crem.at[p], core_peer)
+
+    def own_copy(p):
+        if p < 4:
+            return pltpu.make_async_copy(gd.at[chunk(p), :, c], ld.at[p], lsem.at[p])
+        return pltpu.make_async_copy(gr.at[p - 4, :, :, c], lr.at[p - 4], lsem.at[p])
+
+    def y_copy(p):
+        if p < 4:
+            return remote(cd.at[p, 1 - y], yd.at[p], ysem.at[p], yrem.at[p], y_peer)
+        return remote(cr.at[p - 4, :, 1 - y], yr.at[p - 4], ysem.at[p], yrem.at[p], y_peer)
+
+    def z_copy(p, k):
+        if p < 4:
+            return remote(yd.at[p], zd.at[p], zsem.at[p, 0], zrem.at[0, p], z_peers[p])
+        zz = lax.rem(z + k, 4)
+        return remote(
+            yr.at[p - 4, zz], zr.at[p - 4, k - 1], zsem.at[p, k], zrem.at[p - 3, k - 1], z_peers[k - 1]
+        )
+
+    order = (0, 4, 1, 5, 2, 6, 3, 7, 8, 9, 10, 11)
+    for p in order:
+        core_copy(p).start()
+        own_copy(p).start()
+
+    def after_core(p):
+        own_copy(p).wait()
+        core_copy(p).wait()
+        if p < 4:
+            cd[p] = (cd[p].astype(wide) + ld[p].astype(wide)).astype(low)
+        else:
+            cr[p - 4] = (cr[p - 4].astype(wide) + lr[p - 4].astype(wide)).astype(low)
+        y_copy(p).start()
+
+    def after_y(p):
+        y_copy(p).wait()
+        if p < 4:
+            yd[p] = (yd[p].astype(wide) + cd[p, y].astype(wide)).astype(low)
+            if p < 3:
+                z_copy(p, 0).start()
+        else:
+            yr[p - 4] = (yr[p - 4].astype(wide) + cr[p - 4, :, y].astype(wide)).astype(low)
+            for k in (1, 2, 3):
+                z_copy(p, k).start()
+
+    count = len(order)
+    for i in range(count + 2):
+        if i < count:
+            after_core(order[i])
+        if i >= 2:
+            after_y(order[i - 2])
+    total = yd[3].astype(wide)
+    for p in (0, 1, 2):
+        z_copy(p, 0).wait()
+        total = total + zd[p].astype(wide)
+    od[...] = total
+    for p in order:
+        if p >= 4:
+            total = yr[p - 4, z].astype(wide)
+            for k in (1, 2, 3):
+                z_copy(p, k).wait()
+                total = total + zr[p - 4, k - 1].astype(wide)
+            orr[p - 4] = total
+
+
+def scatter_sums(grads, count):
+    low = jnp.bfloat16
+    w_q, w_k, w_v, w_o, w_u, w_d = [item.astype(low) for item in grads]
+    depth = w_q.shape[0]
+    if count != 16 or depth % (16 * 16) or w_u.shape[1] != 4 * depth:
+        return [
+            lax.psum_scatter(item, "batch", scatter_dimension=0, tiled=True) for item in grads
+        ]
+    rows = depth // 16
+    gd = w_d.reshape(4, 2, 2, 4 * rows, depth)
+    pieces = [w_u[:, i * depth : (i + 1) * depth] for i in range(4)] + [w_o, w_k, w_v, w_q]
+    gr = jnp.stack(pieces).reshape(8, 4, 2, 2, rows, depth)
+    hbm = pl.BlockSpec(memory_space=pl.ANY)
+    vmem = pl.BlockSpec(memory_space=pltpu.VMEM)
+    dma = pltpu.SemaphoreType.DMA
+    down, rest = pl.pallas_call(
+        scatter_kernel,
+        out_shape=[
+            jax.ShapeDtypeStruct((4 * rows, depth), jnp.float32),
+            jax.ShapeDtypeStruct((8, rows, depth), jnp.float32),
+        ],
+        in_specs=[hbm, hbm],
+        out_specs=[vmem, vmem],
+        scratch_shapes=[
+            pltpu.VMEM((4, 2, 4 * rows, depth), low),
+            pltpu.VMEM((8, 4, 2, rows, depth), low),
+            pltpu.VMEM((4, 4 * rows, depth), low),
+            pltpu.VMEM((8, 4, rows, depth), low),
+            pltpu.VMEM((3, 4 * rows, depth), low),
+            pltpu.VMEM((8, 3, rows, depth), low),
+            pltpu.VMEM((4, 2, 4 * rows, depth), low),
+            pltpu.VMEM((8, 4, 2, rows, depth), low),
+            dma((12,)),
+            dma((12,)),
+            dma((12,)),
+            dma((12,)),
+            dma((12, 4)),
+            dma((9, 3)),
+            dma((12,)),
+        ],
+        compiler_params=pltpu.CompilerParams(
+            collective_id=0, has_side_effects=True, vmem_limit_bytes=56 * 2**20
+        ),
+        name="weight_sums",
+    )(gd, gr)
+    up = jnp.concatenate([rest[0], rest[1], rest[2], rest[3]], axis=1)
+    return [rest[7], rest[5], rest[6], rest[4], up, down]
 
 
 def on_device(
@@ -259,13 +404,9 @@
     grad_gain_one = jnp.sum(grad_normed_one * plain_one, axis=(0, 1))
     grad_shift_one = jnp.sum(grad_normed_one, axis=(0, 1))
     grad_inputs = grad_middle + norm_backward(grad_normed_one, plain_one, inverse_one, gain_rows[0])
-    big_sums = (
-        lax.psum_scatter(grad_w_query, "batch", scatter_dimension=0, tiled=True),
-        lax.psum_scatter(grad_w_key, "batch", scatter_dimension=0, tiled=True),
-        lax.psum_scatter(grad_w_value, "batch", scatter_dimension=0, tiled=True),
-        lax.psum_scatter(grad_w_out, "batch", scatter_dimension=0, tiled=True),
-        lax.psum_scatter(grad_w_up, "batch", scatter_dimension=0, tiled=True),
-        lax.psum_scatter(grad_w_down, "batch", scatter_dimension=0, tiled=True),
+    big_sums = scatter_sums(
+        (grad_w_query, grad_w_key, grad_w_value, grad_w_out, grad_w_up, grad_w_down),
+        lax.axis_size("batch"),
     )
     small_sums = lax.psum(
         (

time: 721 us -> 583 us (0.81)
  waiting for transfers between devices: 268 us -> 51.3 us
  Pallas kernels: 0 us -> 92.3 us
  between operations: 17.1 us -> 3.5 us
  local copies, waits for them, and re-layouts: 31.1 us -> 44.4 us
  matrix products: 204 us -> 191 us
    reduce_scatter x6 -> x0, waiting for transfers between devices: 200 us -> none  [the longest x1 116 us: on_device(): lax.psum_scatter(grad_w_up, 'batch', scatter_dimension=0, tiled=True)]
    pallas_call x0 -> x1, Pallas kernels: none -> 92.3 us  [scatter_sums(): pl.pallas_call(scatter_kernel, out_shape=[jax.ShapeDtypeStruct((4 * rows,...]
    ppermute x4, waiting for transfers between devices: 68 us -> 51.3 us  [partner(): return lax.ppermute(block, axis, route)]
    dot_general x6, matrix products: 33.5 us -> 21.6 us  [weight_grad(): jnp.einsum('rsd,rse->de', left, right, preferred_element_type=jnp.float32)]
    unnamed x141 -> x129, local copies, waits for them, and re-layouts: 19.6 us -> 23.2 us
  transfers between devices with their start and end apart: 10 -> 4, of which waited for: 5 -> 2; matrix products, arithmetic and copies ran while one was open for 34% -> 20% of each run, Pallas kernels for 0% -> 0%
where the time goes in v1:
time: 583 us; the launch traced here: 580 us
  matrix products  191 us (33%)
  blocking collectives  99.4 us (17%)
  other arithmetic  92.7 us (16%)
  Pallas kernels  92.3 us (16%)
  waiting for transfers between devices  51.3 us (9%)
  local copies, waits for them, and re-layouts  44.4 us (8%)
    pallas_call x1, Pallas kernels, scatter_sums(): pl.pallas_call(scatter_kernel, out_shape=[jax.ShapeDtypeStruct((4 * rows,...  92.3 us
    psum x1, blocking collectives, on_device(): lax.psum((jnp.stack([grad_gain_one, grad_gain_two]), jnp.stack([grad_shif...  58.3 us
    ppermute x4, waiting for transfers between devices, partner(): return lax.ppermute(block, axis, route)  51.3 us
    reduce_sum x1, other arithmetic, bias_grad(): jnp.sum(grad_wide * (offset == bucket).astype(jnp.float32)[None], axis=(1...  48.6 us
    dot_general x1, matrix products, score_block(): jnp.einsum('ihd,jhd->hij', heads_of(query[row_index]), heads_of(far_keys[...  44.3 us
    psum x1, blocking collectives, on_device(): lax.psum((jnp.sum(own_valid * jnp.sum(block_out * block_out, axis=-1)), j...  41.1 us
    dot_general x6, matrix products, back_project(): jnp.einsum('rse,de->rsd', grad_low, weight, preferred_element_type=jnp.fl...  29.8 us
    dot_general x6, matrix products, project(): jnp.einsum('rsd,de->rse', left, right, preferred_element_type=jnp.float32)  29 us
  transfers between devices with their start and end apart: 4, of which 2 were waited for; matrix products, arithmetic and copies ran while one was open for 20% of the time, Pallas kernels for 0%

profile of v1, /device:TPU:0, one launch (start us, length us, event | category | flops | bytes accessed | tf_op | source)
XLA Modules:
  0.0 579.6 jit_solution(2957528170962146527)
XLA Ops:
  0.7 2.0 reduce_sum.319
  4.8 2.1 fusion.72
  6.9 2.9 collective-permute-start
  9.9 2.1 fusion.73
  13.2 2.1 copy.47
  15.3 2.6 convert_reduce_fusion.1
  17.9 2.0 copy.51
  21.2 1.3 broadcast_in_dim.48
  25.1 3.9 convolution_convert_fusion.8
  29.6 1.3 compare_or_fusion
  30.8 6.6 %fusion.52 = (f32[768,768]{0,1:T(8,128)S(1)}, f32[768,768]{0,1:T(8,128)}, f32[768,768]{0,1:T(8,128)}, f32[768,768]{0,1:T(8,128)}, f32[768,768]{0,1:T(8,128)}, /*index=5*/f32[768,768]{0,1:T(8,128)}, f32[768,768]{0,1:T(8,128)}) fusion(s32[768]{0:T(1024)S(1)} %get-tuple-element.138, s32[768]{0:T(1024)S(1)} %get-tuple-element.137), kind=kLoop, calls=%fused_computation.98 | loop fusion | flops 10027008 | bytes 16521216 | tf_op jit(solution)/shard_map/convert_element_type | solution.py:48
  37.4 7.2 %fusion.59 = (f32[768,768]{0,1:T(8,128)}, f32[768,768]{0,1:T(8,128)}, f32[768,768]{0,1:T(8,128)}, f32[768,768]{0,1:T(8,128)}, f32[768,768]{0,1:T(8,128)}, /*index=5*/f32[768,768]{0,1:T(8,128)}, f32[768,768]{0,1:T(8,128)}) fusion(s32[768]{0:T(1024)S(1)} %get-tuple-element.153, s32[768]{0:T(1024)S(1)} %get-tuple-element.154), kind=kLoop, calls=%fused_computation.105 | loop fusion | flops 10027008 | bytes 16521216 | tf_op jit(solution)/shard_map/convert_element_type | solution.py:48
  44.6 16.8 %collective-permute-done.1 = bf16[1,768,768]{2,1,0:T(8,128)(2,1)} collective-permute-done((bf16[1,768,768]{2,1,0:T(8,128)(2,1)}, bf16[1,768,768]{2,1,0:T(8,128)(2,1)}, u32[]{:S(2)}, u32[]{:S(2)}) %collective-permute-start.1) | collective-permute-done | bytes 1179680 | tf_op jit(solution)/shard_map/ppermute | solution.py:22
  61.4 2.4 copy.49
  63.8 44.3 %fusion.117 = (f32[12,768]{1,0:T(8,128)}, f32[12,768,768]{1,2,0:T(8,128)}) fusion(f32[768,768]{0,1:T(8,128)} %get-tuple-element.131, f32[12]{0:T(128)} %get-tuple-element.88, f32[768,768]{0,1:T(8,128)} %get-tuple-element.132, f32[12]{0:T(128)} %get-tuple-element.89, f32[768,768]{0,1:T(8,128)} %get-tuple-element.133, f32[12]{0:T(128)S(1)} %copy-done.50, ...), kind=kOutput, calls=%fused_computation.236 | convolution fusion | flops 1125374976 | bytes 64328352 | tf_op jit(solution)/shard_map/ihd,jhd->hij/dot_general | solution.py:278
  108.1 12.9 %fusion.14 = f32[12,768]{1,0:T(8,128)S(1)} fusion(f32[12,768,768]{1,2,0:T(8,128)} %get-tuple-element.142, f32[12,768]{1,0:T(8,128)} %get-tuple-element.141), kind=kLoop, calls=%fused_computation.34 | loop fusion | flops 14146560 | bytes 28385280 | tf_op jit(solution)/shard_map/reduce_sum | solution.py:298
  121.6 1.6 copy.48
  123.2 11.8 %multiply_convert_fusion.4 = bf16[12,64,768]{2,1,0:T(8,128)(2,1)S(1)} fusion(bf16[768,12,64]{0,2,1:T(8,128)(2,1)S(1)} %bitcast.183, f32[12,768,768]{1,2,0:T(8,128)} %get-tuple-element.142, f32[12,768]{1,0:T(8,128)S(1)} %fusion.14, f32[12,768]{1,0:T(8,128)S(1)} %copy-done.27, f32[768]{0:T(1024)S(1)} %copy-done.37), kind=kOutput, calls=%fused_computation.80 | convolution fusion | flops 928382976 | bytes 30747648 | tf_op jit(solution)/shard_map/hij,jhd->ihd/dot_general | solution.py:300
  135.1 2.7 fusion.114
  138.7 4.2 fusion.33
  142.9 7.5 %convolution_convert_fusion.1 = bf16[3072,768]{1,0:T(8,128)(2,1)} fusion(f32[1,1,768,768]{3,2,1,0:T(8,128)S(1)} %copy-done.7, f32[768,3072]{1,0:T(8,128)S(1)} %fusion.33, f32[3072]{0:T(1024)S(1)} %bitcast.214), kind=kOutput, calls=%fused_computation.51 | convolution fusion | flops 3650420736 | bytes 16527360 | tf_op jit(solution)/shard_map/rsd,rse->de/dot_general | solution.py:67
  150.4 13.3 %convert_reduce_fusion = (f32[3072]{0:T(1024)}, bf16[768,3072]{1,0:T(8,128)(2,1)}) fusion(f32[768,3072]{1,0:T(8,128)S(1)} %fusion.33, f32[3072]{0:T(1024)S(1)} %bitcast.215, bf16[1,3072,768]{2,1,0:T(8,128)(2,1)} %param.26, f32[1,1,768,768]{3,2,1,0:T(8,128)S(1)} %copy-done.7), kind=kOutput, calls=%fused_computation.48 | convolution fusion | flops 3678729216 | bytes 21258240 | tf_op jit(solution)/shard_map/rse,de->rsd/dot_general | solution.py:71
  163.7 8.3 %fusion.118 = (f32[768]{0:T(1024)}, f32[768,768]{1,0:T(8,128)}) fusion(bf16[768,3072]{1,0:T(8,128)(2,1)} %get-tuple-element.150, bf16[1,768,3072]{2,1,0:T(8,128)(2,1)S(1)} %bitcast.180), kind=kOutput, calls=%fused_computation.237 | convolution fusion | flops 3624467712 | bytes 11799552 | tf_op jit(solution)/shard_map/rse,de->rsd/dot_general | solution.py:71
  172.1 5.7 convolution_convert_fusion
  177.8 3.1 copy.52
  180.9 13.9 %multiply_reduce_fusion.2 = (f32[768]{0:T(1024)}, f32[768]{0:T(1024)}, f32[768]{0:T(1024)S(1)}, f32[768]{0:T(1024)S(1)}, f32[768]{0:T(1024)}, /*index=5*/f32[1,1,768,768]{2,3,1,0:T(8,128)}) fusion(f32[768,768]{0,1:T(8,128)S(1)} %get-tuple-element.107, f32[768]{0:T(1024)S(1)} %copy-done.45, f32[768,768]{0,1:T(8,128)} %get-tuple-element.143, ...), kind=kOutput, calls=%fused_computation.68 | convolution fusion | flops 3656315136 | bytes 23632896 | tf_op jit(solution)/shard_map/rsd,de->rse/dot_general | solution.py:63
  198.1 12.6 %fusion.68 = bf16[12,64,768]{2,1,0:T(8,128)(2,1)} fusion(bf16[768,12,64]{0,2,1:T(8,128)(2,1)S(1)} %bitcast.181, f32[12,768,768]{1,2,0:T(8,128)} %get-tuple-element.142, f32[12,768]{1,0:T(8,128)S(1)} %copy-done.26), kind=kOutput, calls=%fused_computation.125 | convolution fusion | flops 920715264 | bytes 30707712 | tf_op jit(solution)/shard_map/hij,ihd->jhd/dot_general | solution.py:386
  210.7 22.3 %multiply_reduce_fusion = (f32[12,768]{1,0:T(8,128)}, f32[12,768,768]{1,2,0:T(8,128)}) fusion(f32[12,768,768]{1,2,0:T(8,128)} %get-tuple-element.142, f32[12,768]{1,0:T(8,128)} %log_add_fusion, bf16[768,12,64]{0,2,1:T(8,128)(2,1)} %bitcast.182, bf16[768,12,64]{0,2,1:T(8,128)(2,1)} %bitcast.184), kind=kOutput, calls=%fused_computation.29 | convolution fusion | flops 927194112 | bytes 59056128 | tf_op jit(solution)/shard_map/ihd,jhd->hij/dot_general | solution.py:352
  233.0 48.6 %fusion.13 = (f32[12]{0:T(128)}, f32[12]{0:T(128)}, f32[12]{0:T(128)}, f32[12]{0:T(128)}, f32[12]{0:T(128)}, /*index=5*/f32[12]{0:T(128)}, f32[12]{0:T(128)}, f3...) fusion(f32[768,768]{0,1:T(8,128)} %get-tuple-element.131, ...), kind=kLoop, calls=%fused_computation.27 | loop fusion | flops 233570096 | bytes 103883424 | tf_op jit(solution)/shard_map/reduce_sum | solution.py:56
  281.6 10.8 %multiply_convert_fusion.2 = bf16[12,64,768]{2,1,0:T(8,128)(2,1)} fusion(bf16[768,12,64]{0,2,1:T(8,128)(2,1)} %bitcast.188, bf16[12,768,768]{1,2,0:T(8,128)(2,1)} %get-tuple-element.105), kind=kOutput, calls=%fused_computation.75 | convolution fusion | flops 907149312 | bytes 16515072 | tf_op jit(solution)/shard_map/hij,ihd->jhd/dot_general | solution.py:378
  292.5 8.7 %multiply_convert_fusion.3 = bf16[12,64,768]{2,1,0:T(8,128)(2,1)} fusion(bf16[768,12,64]{0,2,1:T(8,128)(2,1)S(1)} %bitcast.173, bf16[12,768,768]{1,2,0:T(8,128)(2,1)} %get-tuple-element.105), kind=kOutput, calls=%fused_computation.76 | convolution fusion | flops 907149312 | bytes 16515072 | tf_op jit(solution)/shard_map/hij,jhd->ihd/dot_general | solution.py:369
  301.2 4.1 fusion.116
  305.9 41.1 %all-reduce = (f32[]{:T(128)}, f32[]{:T(128)}, f32[]{:T(128)}) all-reduce(f32[]{:T(128)} %get-tuple-element.93, f32[]{:T(128)} %get-tuple-element.94, f32[]{:T(128)} %get-tuple-element.92), channel_id=1, replica_groups=mesh['stream'=2,'batch'=16] {'stream','batch'}, use_global_device_ids=true, to_apply=%region_43.44 | all-reduce | flops 3 | bytes 24 | tf_op jit(solution)/shard_map/psum | solution.py:318
  349.7 2.3 collective-permute-start.3
  351.9 3.2 copy.60
  359.6 1.4 concatenate.8
  361.0 2.4 convolution_convert_fusion.6
  367.8 34.5 %collective-permute-done.2 = bf16[1,768,768]{1,2,0:T(8,128)(2,1)} collective-permute-done((bf16[1,768,768]{1,2,0:T(8,128)(2,1)}, bf16[1,768,768]{1,2,0:T(8,128)(2,1)}, u32[]{:S(2)}, u32[]{:S(2)}) %collective-permute-start.2) | collective-permute-done | bytes 1179680 | tf_op jit(solution)/shard_map/ppermute | solution.py:22
  402.3 2.4 convolution_convert_fusion.5
  405.9 2.4 convolution_convert_fusion.4
  410.6 92.3 %weight_sums.1 = (f32[192,768]{1,0:T(8,128)}, f32[8,48,768]{2,1,0:T(8,128)}) custom-call(bf16[4,2,2,192,768]{4,3,2,1,0:T(8,128)(2,1)} %bitcast.178, bf16[8,4,2,2,48,768]{5,4,3,2,1,0:T(8,128)(2,1)} %constant_dynamic-update-slice_fusion.gr), custom_call_target="tpu_custom_call" | custom-call | tf_op jit(solution)/shard_map/weight_sums/pallas_call | solution.py:183
  502.8 2.4 slice_bitcast_fusion.3
  505.3 2.5 fusion.78
  507.9 3.4 multiply_reduce_fusion.4
  513.2 2.0 copy.61
  516.5 58.3 %all-reduce.1 = (f32[1,2,768]{2,1,0:T(2,128)}, f32[1,2,768]{2,1,0:T(2,128)}, f32[1,3072]{1,0:T(1,128)}, f32[1,768]{1,0:T(1,128)}, f32[1,14,12]{2,1,0:T(8,128)S(1)}) all-reduce(f32[1,2,768]{2,1,0:T(2,128)S(1)} %maximum_bitcast_fusion.1, f32[1,2,768]{2,1,0:T(2,128)S(1)} %maximum_bitcast_fusion.2, ...), channel_id=1, replica_groups=mesh['stream'=2,'batch'=16] {'batch'}, use_global_device_ids=true, to_apply=%region_13.14 | all-reduce | flops 7080 | bytes 56640 | tf_op jit(solution)/shard_map/psum | solution.py:411
  575.5 2.0 maximum_bitcast_fusion
  577.5 1.9 copy.78
  (164 shorter events, 29.9 us)
Async XLA Ops:
  0.6 134.4 %copy-start = (bf16[1,768,768]{2,1,0:T(8,128)(2,1)S(1)}, bf16[1,768,768]{2,1,0:T(8,128)(2,1)}, u32[]{:S(2)}) copy-start(bf16[1,768,768]{2,1,0:T(8,128)(2,1)} %param.23) | copy-start | bytes 3538948
  0.7 2.5 copy-start.1
  3.6 3.3 copy-start.32
  3.6 3.3 copy-start.30
  4.8 5.1 copy-start.23
  4.8 5.1 copy-start.52
  6.9 5.1 copy-start.34
  6.9 114.7 %collective-permute-start = (bf16[1,768,768]{2,1,0:T(8,128)(2,1)}, bf16[1,768,768]{2,1,0:T(8,128)(2,1)}, u32[]{:S(2)}, u32[]{:S(2)}) collective-permute-start(bf16[1,768,768]{2,1,0:T(8,128)(2,1)} %fusion.72), channel_id=1, source_target_pairs={{0,16},{16,0},{1,17},{17,1},{2,18},{18,2},{3,19},{19,3},{4,20},{20... | collective-permute-start | bytes 3538952 | tf_op jit(solution)/shard_map/ppermute | solution.py:22
  12.0 49.4 %collective-permute-start.1 = (bf16[1,768,768]{2,1,0:T(8,128)(2,1)}, bf16[1,768,768]{2,1,0:T(8,128)(2,1)}, u32[]{:S(2)}, u32[]{:S(2)}) collective-permute-start(bf16[1,768,768]{2,1,0:T(8,128)(2,1)} %fusion.73), channel_id=1, source_target_pairs={{0,16},{16,0},{1,17},{17,1},{2,18},{18,2},{3,19},{19,3},{4,20},{20... | collective-permute-start | bytes 3538952 | tf_op jit(solution)/shard_map/ppermute | solution.py:22
  15.3 2.6 copy-start.6
  17.9 4.5 copy-start.20
  25.1 3.9 copy-start.46
  25.1 4.5 copy-start.36
  37.4 26.4 %copy-start.4 = (f32[768,768]{0,1:T(8,128)}, f32[768,768]{0,1:T(8,128)S(1)}, u32[]{:S(2)}) copy-start(f32[768,768]{0,1:T(8,128)S(1)} %get-tuple-element.123) | copy-start | bytes 7077892
  44.6 19.2 %copy-start.49 = (f32[12]{0:T(128)S(1)}, f32[12]{0:T(128)}, u32[]{:S(2)}) copy-start(f32[12]{0:T(128)} %get-tuple-element.76) | copy-start | bytes 148
  44.6 19.2 %copy-start.50 = (f32[12]{0:T(128)S(1)}, f32[12]{0:T(128)}, u32[]{:S(2)}) copy-start(f32[12]{0:T(128)} %get-tuple-element.77) | copy-start | bytes 148
  108.1 12.9 %copy-start.27 = (f32[12,768]{1,0:T(8,128)S(1)}, f32[12,768]{1,0:T(8,128)}, u32[]{:S(2)}) copy-start(f32[12,768]{1,0:T(8,128)} %get-tuple-element.141) | copy-start | bytes 110596
  123.2 11.9 %copy-start.18 = (bf16[1,768,768]{1,2,0:T(8,128)(2,1)}, bf16[1,768,768]{1,2,0:T(8,128)(2,1)S(1)}, u32[]{:S(2)}) copy-start(bf16[1,768,768]{1,2,0:T(8,128)(2,1)S(1)} %copy.48) | copy-start | bytes 3538948
  123.2 11.9 %copy-start.2 = (f32[1,1,768,768]{2,3,1,0:T(8,128)S(1)}, f32[1,1,768,768]{2,3,1,0:T(8,128)}, u32[]{:S(2)}) copy-start(f32[1,1,768,768]{2,3,1,0:T(8,128)} %copy.47) | copy-start | bytes 7077892
  135.1 2.8 copy-start.25
  135.1 3.5 slice-start
  135.1 3.6 slice-start.1
  138.7 4.2 copy-start.7
  138.7 4.3 copy-start.54
  142.9 7.5 %copy-start.8 = (f32[768,3072]{1,0:T(8,128)}, f32[768,3072]{1,0:T(8,128)S(1)}, u32[]{:S(2)}) copy-start(f32[768,3072]{1,0:T(8,128)S(1)} %fusion.33) | copy-start | bytes 28311556
  163.7 8.4 %copy-start.55 = (bf16[768,3072]{1,0:T(8,128)(2,1)S(1)}, bf16[768,3072]{1,0:T(8,128)(2,1)}, u32[]{:S(2)}) copy-start(bf16[768,3072]{1,0:T(8,128)(2,1)} %get-tuple-element.150) | copy-start | bytes 14155780
  177.8 3.1 copy-start.45
  180.9 13.9 %copy-start.9 = (f32[1,1,768,768]{2,3,1,0:T(8,128)S(1)}, f32[1,1,768,768]{2,3,1,0:T(8,128)}, u32[]{:S(2)}) copy-start(f32[1,1,768,768]{2,3,1,0:T(8,128)} %copy.51) | copy-start | bytes 7077892
  180.9 13.9 %copy-start.10 = (f32[768,768]{0,1:T(8,128)S(1)}, f32[768,768]{0,1:T(8,128)}, u32[]{:S(2)}) copy-start(f32[768,768]{0,1:T(8,128)} %copy.52) | copy-start | bytes 7077892
  195.7 2.5 copy-start.26
  210.7 22.3 %copy-start.5 = (f32[768,768]{0,1:T(8,128)S(1)}, f32[768,768]{0,1:T(8,128)}, u32[]{:S(2)}) copy-start(f32[768,768]{0,1:T(8,128)} %copy-done.4) | copy-start | bytes 7077892
  281.6 10.8 %copy-start.14 = (bf16[1,768,768]{1,2,0:T(8,128)(2,1)S(1)}, bf16[1,768,768]{1,2,0:T(8,128)(2,1)}, u32[]{:S(2)}) copy-start(bf16[1,768,768]{1,2,0:T(8,128)(2,1)} %copy.49) | copy-start | bytes 3538948
  292.5 8.7 %copy-start.42 = (f32[768]{0:T(1024)S(1)}, f32[768]{0:T(1024)}, u32[]{:S(2)}) copy-start(f32[768]{0:T(1024)} %get-tuple-element.147) | copy-start | bytes 9220
  301.1 4.2 copy-start.35
  301.1 4.2 copy-start.43
  301.2 4.2 copy-start.44
  301.2 47.9 %copy-start.41 = (f32[768]{0:T(1024)S(1)}, f32[768]{0:T(1024)}, u32[]{:S(2)}) copy-start(f32[768]{0:T(1024)} %get-tuple-element.70) | copy-start | bytes 9220
  349.7 56.2 %collective-permute-start.3 = (bf16[1,768,768]{1,2,0:T(8,128)(2,1)}, bf16[1,768,768]{1,2,0:T(8,128)(2,1)}, u32[]{:S(2)}, u32[]{:S(2)}) collective-permute-start(bf16[1,768,768]{1,2,0:T(8,128)(2,1)} %bitcast.189), channel_id=1, source_target_pairs={{0,16},{16,0},{1,17},{17,1},{2,18},{18,2},{3,19},{19,3},{4,20},{20... | collective-permute-start | bytes 3538952 | tf_op jit(solution)/shard_map/ppermute | solution.py:22
  356.2 46.1 %collective-permute-start.2 = (bf16[1,768,768]{1,2,0:T(8,128)(2,1)}, bf16[1,768,768]{1,2,0:T(8,128)(2,1)}, u32[]{:S(2)}, u32[]{:S(2)}) collective-permute-start(bf16[1,768,768]{1,2,0:T(8,128)(2,1)} %bitcast.24), channel_id=1, source_target_pairs={{0,16},{16,0},{1,17},{17,1},{2,18},{18,2},{3,19},{19,3},{4,20},{20... | collective-permute-start | bytes 3538952 | tf_op jit(solution)/shard_map/ppermute | solution.py:22
  357.4 3.6 copy-start.12
  502.8 2.5 copy-start.53
  505.3 2.6 copy-start.3
  505.3 2.6 copy-start.22
  505.3 2.6 copy-start.29
  505.3 2.6 copy-start.31
  505.3 2.6 copy-start.33
  507.9 4.6 copy-start.13
  513.2 3.4 copy-start.38
  (14 other events, 21.2 us)

commit v2 on v0

v2 whole, which is shorter than its diff:
```python
import functools

import jax
import jax.numpy as jnp
from jax import lax
from jax.experimental import pallas as pl
from jax.experimental.pallas import tpu as pltpu
from jax.sharding import PartitionSpec as P

GRID = 16
PAGES = 3
MESH = pl.DeviceIdType.MESH
LOG2E = 1.4426950408889634
LN2 = 0.6931471805599453
GELU_IN = 0.7978845608028654
GELU_CUBE = 0.044715
masked_fill = -1e30
f32 = jnp.float32
bf16 = jnp.bfloat16


def dot(left, right, form="nn"):
    dims = {"nn": (1, 0), "nt": (1, 1), "tn": (0, 0)}[form]
    return lax.dot_general(
        left, right, (((dims[0],), (dims[1],)), ((), ())), preferred_element_type=f32
    )


def plain_norm(values):
    center = values - jnp.mean(values, axis=-1, keepdims=True)
    inverse = lax.rsqrt(jnp.mean(center * center, axis=-1, keepdims=True) + 1e-05)
    return center * inverse, inverse


def norm_backward(grad_normed, plain, inverse, gain_row):
    scaled = grad_normed * gain_row
    first_mean = jnp.mean(scaled, axis=-1, keepdims=True)
    second_mean = jnp.mean(scaled * plain, axis=-1, keepdims=True)
    return inverse * (scaled - first_mean - plain * second_mean)


def head_rows(first, half, width):
    empty = jnp.zeros((half.shape[0], width), half.dtype)
    return [half, empty] if first else [empty, half]


def attend_kernel(
    normed, far, wq, wk, wv, feat, bias, valid_row, q_o, k_o, v_o, att_o, lse_o, q_t, v_t, att_t
):
    width = normed.shape[1]
    slots = normed.shape[0]
    heads = bias.shape[0]
    size = width // heads
    q_o[...] = (dot(normed[...], wq[...]) * (LOG2E * size**-0.5)).astype(bf16)
    q_t[...] = q_o[...].T
    k_o[...] = dot(far[...], wk[...]).astype(bf16)
    v_o[...] = dot(far[...], wv[...]).astype(bf16)
    v_t[...] = v_o[...].T
    ones = jnp.ones((16, slots), bf16)
    pad = jnp.zeros((2 * size - bias.shape[1], slots), bf16)

    def pair(p, carry):
        start = pl.multiple_of(p * 2 * size, 2 * size)
        left = jnp.concatenate([k_o[:, pl.ds(start, 2 * size)], feat[...]], axis=1)
        for hh in range(2):
            rows = pl.ds(pl.multiple_of(start + hh * size, size), size)
            right = jnp.concatenate(
                head_rows(hh == 0, q_t[rows, :], slots) + [bias[2 * p + hh], pad], axis=0
            )
            scores = dot(left, right)
            top = jnp.max(scores, axis=0, keepdims=True)
            weight = jnp.exp2(scores - top).astype(bf16)
            found = dot(jnp.concatenate([v_t[rows, :], ones], axis=0), weight)
            total = found[size : size + 1]
            att_t[rows, :] = (found[:size] * (valid_row[...] / total)).astype(bf16)
            lse_o[2 * p + hh] = top + jnp.log2(total)
        return carry

    lax.fori_loop(0, heads // 2, pair, 0)
    att_o[...] = att_t[...].T


SLOT = {
    name: i
    for i, name in enumerate(
        ("att", "wo", "n2", "n2t", "g2", "wu0", "wu1", "wd0", "wd1", "sd0", "sd1", "sr0", "sr1", "q", "k", "v", "back")
    )
}
SLOT.update(act=13, gp=14, gm=2, go=3, got=4, far=5, q_t=6, k_t=7, dk=8, so=9, send=10, dv=11)
SLOT.update(normed=0, wq=1, wv=2, wk=12, dq=13, sk=6, sv=7, sq=3, dq_t=8)


def layer_kernel(
    x, cot, att, q, k, v, normed, far, wq, wk, wv, wo, wup, wdn,
    lse, up_bias, down_bias, gains, shifts, valid_col, valid_row, feat, feat_t, bias, offsets,
    block_o, grad_o, down_o, up_o, wo_o, wq_o, wk_o, wv_o, gains_o, shifts_o, down_bias_o, up_bias_o, table_o,
    pool, wide, delta, cells, cd, cr, yd, yr, zd, zr, hop, hop_in, sums, sums_in, table_in,
    in_sem, w_sem, out_sem, csem, crem, ysem, yrem, zsem, zrem, xsem, xrem, hsem, hrem, asem, arem, bsem, brem,
):
    slots, width = x.shape
    heads = bias.shape[0]
    size = width // heads
    st = lax.axis_index("stream")
    me = lax.axis_index("batch")
    c = lax.rem(me, 2)
    y = lax.rem(lax.div(me, 2), 2)
    z = lax.div(me, 4)
    core_peer = (st, me + 1 - 2 * c)
    y_peer = (st, me + 2 - 4 * y)
    z_at = [lax.rem(z + i, 4) for i in range(4)]
    z_peers = [(st, z_at[i] * 4 + y * 2 + c) for i in range(4)]
    x_peer = (1 - st, me)
    one_peer = (st, me + 4 - 8 * lax.rem(z, 2))
    two_peer = (st, me + 8 - 16 * lax.div(z, 2))

    def slot(name):
        return pool.at[SLOT[name]]

    def remote(source, target, send, recv, peer):
        return pltpu.make_async_remote_copy(
            source, target, send, recv, device_id=peer, device_id_type=MESH
        )

    singles = dict(
        x=(x, wide.at[0]), cot=(cot, wide.at[1]), att=(att, slot("att")), wo=(wo, slot("wo")),
        q=(q, slot("q")), k=(k, slot("k")), v=(v, slot("v")), wk=(wk, slot("wk")), wv=(wv, slot("wv")),
        far=(far, slot("far")), normed=(normed, slot("normed")), wq=(wq, slot("wq")),
    )
    load_at = {name: i for i, name in enumerate(singles)}

    def load(name):
        return pltpu.make_async_copy(*singles[name], in_sem.at[load_at[name]])

    def chunk_of(t):
        return lax.rem(z + t + 1, 4)

    def chunk_loads(t):
        at = pl.multiple_of(chunk_of(t) * width, width)
        two = lax.rem(t, 2)
        return (
            pltpu.make_async_copy(
                wup.at[:, pl.ds(at, width)], pool.at[SLOT["wu0"] + two], w_sem.at[two, 0]
            ),
            pltpu.make_async_copy(
                wdn.at[pl.ds(at, width), :], pool.at[SLOT["wd0"] + two], w_sem.at[two, 1]
            ),
        )

    for name in ("att", "wo", "x", "cot"):
        load(name).start()
    for copy in chunk_loads(0):
        copy.start()

    barrier = pltpu.get_barrier_semaphore()
    peers = [core_peer, y_peer, x_peer] + z_peers[1:]
    for peer in peers:
        pl.semaphore_signal(barrier, inc=1, device_id=peer, device_id_type=MESH)
    pl.semaphore_wait(barrier, len(peers))

    def down_view(at):
        return pool.at[at].reshape(2, 2, width // 4, width)

    def rest_view(at):
        return pool.at[at].reshape(4, 2, 2, width // 16, width)

    def core_down(t):
        at = SLOT["sd0"] + lax.rem(t, 2)
        return remote(down_view(at).at[:, 1 - c], cd.at[t], csem.at[t], crem.at[t], core_peer)

    def core_rest(p, at):
        return remote(
            rest_view(at).at[:, :, 1 - c], cr.at[p], csem.at[4 + p], crem.at[4 + p], core_peer
        )

    def y_down(t):
        return remote(cd.at[t, 1 - y], yd.at[t], ysem.at[t], yrem.at[t], y_peer)

    def y_rest(p):
        return remote(cr.at[p, :, 1 - y], yr.at[p], ysem.at[4 + p], yrem.at[4 + p], y_peer)

    def z_down(t):
        return remote(yd.at[t], zd.at[t], zsem.at[0, t], zrem.at[0, t], z_peers[t + 1])

    def z_rest(p, i):
        q = chunk_of(p) if p < 4 else p
        return remote(
            yr.at[p, z_at[i]], zr.at[q, i - 1], zsem.at[1 + p, i - 1], zrem.at[1 + q, i - 1], z_peers[i]
        )

    def z_here(q, i):
        return remote(
            yr.at[q, z_at[i]], zr.at[q, i - 1], zsem.at[1 + q, i - 1], zrem.at[1 + q, i - 1], z_peers[i]
        )

    def add_low(left, right):
        return (left.astype(f32) + right.astype(f32)).astype(bf16)

    def after_core_down(t):
        core_down(t).wait()
        cd[t] = add_low(cd[t], down_view(SLOT["sd0"] + lax.rem(t, 2))[:, c])
        y_down(t).start()

    def after_core_rest(p, at):
        core_rest(p, at).wait()
        cr[p] = add_low(cr[p], rest_view(at)[:, :, c])
        y_rest(p).start()

    def after_y_down(t):
        y_down(t).wait()
        yd[t] = add_low(yd[t], cd[t, y])
        if t < 3:
            z_down(t).start()

    def after_y_rest(p):
        y_rest(p).wait()
        yr[p] = add_low(yr[p], cr[p, :, y])
        for i in (1, 2, 3):
            z_rest(p, i).start()

    def end_down():
        total = yd[3].astype(f32)
        for t in range(3):
            z_down(t).wait()
            total = total + zd[t].astype(f32)
        down_o[...] = total

    def end_rest(q):
        held = lax.rem(q - z + 3, 4) if q < 4 else q
        total = yr[held, z].astype(f32)
        for i in (1, 2, 3):
            z_here(q, i).wait()
            total = total + zr[q, i - 1].astype(f32)
        return total

    load("att").wait()
    load("wo").wait()
    load("x").wait()
    load("cot").wait()
    sums[...] = jnp.zeros_like(sums)
    third = slots // 3
    spans = [pl.ds(part * third, third) for part in range(3)]
    for span in spans:
        middle = wide[0, span, :] + dot(pool[SLOT["att"], span, :], pool[SLOT["wo"]])
        wide[2, span, :] = middle
        wide[3, span, :] = middle + down_bias[...]
        plain, inverse = plain_norm(middle)
        pool[SLOT["n2"], span, :] = (plain * gains[1:2, :] + shifts[1:2, :]).astype(bf16)
        low = wide[1, span, :].astype(bf16)
        pool[SLOT["g2"], span, :] = low
        sums[4:5, :] += jnp.sum(low.astype(f32), axis=0, keepdims=True)
    pool[SLOT["n2t"]] = pool[SLOT["n2"]].T
    wide[4] = jnp.zeros((slots, width), f32)

    def feed(t, carry):
        two = lax.rem(t, 2)
        at = chunk_of(t)
        for copy in chunk_loads(t):
            copy.wait()

        @pl.when(t < 3)
        def _():
            for copy in chunk_loads(t + 1):
                copy.start()

        w_u = pool.at[SLOT["wu0"] + two]
        w_d = pool.at[SLOT["wd0"] + two]
        for part in range(3):
            cols = slice(part * third, (part + 1) * third)
            pre = dot(pool[SLOT["n2"]], w_u[:, cols]) + up_bias[at, :, cols]
            grad_act = dot(pool[SLOT["g2"]], w_d[cols, :], "nt")
            square = pre * pre
            gate = jnp.tanh(pre * (GELU_IN + (GELU_IN * GELU_CUBE) * square))
            gate_half = 0.5 + 0.5 * gate
            pool[SLOT["act"], :, cols] = (pre * gate_half).astype(bf16)
            slope = pre * (GELU_IN + (3.0 * GELU_IN * GELU_CUBE) * square)
            grad_pre = (grad_act * (gate_half * (1.0 + (1.0 - gate) * slope))).astype(bf16)
            pool[SLOT["gp"], :, cols] = grad_pre
            sums[pl.ds(5 + at, 1), cols] = jnp.sum(grad_pre.astype(f32), axis=0, keepdims=True)
        pool[SLOT["sd0"] + two] = dot(pool[SLOT["act"]], pool[SLOT["g2"]], "tn").astype(bf16)
        core_down(t).start()

        @pl.when(t > 0)
        def _():
            after_core_rest(t - 1, SLOT["sr0"] + 1 - two)

        pool[SLOT["sr0"] + two] = dot(pool[SLOT["n2t"]], pool[SLOT["gp"]]).astype(bf16)
        core_rest(t, SLOT["sr0"] + two).start()
        wide[3] = wide[3] + dot(pool[SLOT["act"]], w_d[...])
        after_core_down(t)
        wide[4] = wide[4] + dot(pool[SLOT["gp"]], w_u[...], "nt")
        return carry

    lax.fori_loop(0, 4, feed, 0)
    after_core_rest(3, SLOT["sr1"])
    for name in ("far", "q", "k", "v"):
        load(name).start()

    pltpu.make_async_copy(wide.at[3], block_o, out_sem.at[0]).start()
    cells[168:176, :] = jnp.zeros((8, width), f32)
    cells[170:171, :] = valid_row[...]
    for span in spans:
        block = wide[3, span, :]
        own = valid_col[span, :]
        sub = block - wide[0, span, :]
        cells[168:169, :] += jnp.sum(own * block * block, axis=0, keepdims=True)
        cells[169:170, :] += jnp.sum(own * sub * sub, axis=0, keepdims=True)
        plain, inverse = plain_norm(wide[2, span, :])
        grad_two = wide[4, span, :]
        sums[1:2, :] += jnp.sum(grad_two * plain, axis=0, keepdims=True)
        sums[3:4, :] += jnp.sum(grad_two, axis=0, keepdims=True)
        middle = wide[1, span, :] + norm_backward(grad_two, plain, inverse, gains[1:2, :])
        wide[2, span, :] = middle
        pool[SLOT["gm"], span, :] = middle.astype(bf16)
    pool[SLOT["so"]] = dot(pool[SLOT["att"]], pool[SLOT["gm"]], "tn").astype(bf16)
    core_rest(4, SLOT["so"]).start()
    own = valid_col[...].astype(bf16)
    pool[SLOT["go"]] = dot(pool[SLOT["gm"]], pool[SLOT["wo"]], "nt").astype(bf16) * own
    pool[SLOT["got"]] = pool[SLOT["go"]].T
    pool[SLOT["q_t"]] = pool[SLOT["att"]].T
    group = 4 * size
    for i in range(heads // 4):
        rows = slice(i * group, (i + 1) * group)
        both = pool[SLOT["q_t"], rows, :].astype(f32) * pool[SLOT["got"], rows, :].astype(f32)
        delta[4 * i : 4 * i + 4] = jnp.sum(both.reshape(4, size, slots), axis=1, keepdims=True)
    after_core_rest(4, SLOT["so"])
    after_y_down(0)
    after_y_rest(0)
    for name in ("normed", "wq", "wk", "wv"):
        load(name).start()
    pltpu.make_async_copy(wide.at[3], block_o, out_sem.at[0]).wait()

    for name in ("q", "k", "v"):
        load(name).wait()
    pool[SLOT["q_t"]] = pool[SLOT["q"]].T
    pool[SLOT["k_t"]] = pool[SLOT["k"]].T
    pad = jnp.zeros((2 * size - bias.shape[1], slots), bf16)
    stride = size + 2 * GRID
    dq_acc = wide.at[pl.ds(3, 2)].reshape(2 * slots, width)
    lane = lax.broadcasted_iota(jnp.int32, (third, 2 * size), 1)
    for part in range(3):
        span = spans[part]

        def pair(p, carry):
            start = pl.multiple_of(p * 2 * size, 2 * size)
            pair_cols = pl.ds(start, 2 * size)
            left = jnp.concatenate([pool[SLOT["k"], span, pair_cols], feat[span, :]], axis=1)
            v_pair = pool[SLOT["v"], span, pair_cols]
            go_pair = pool[SLOT["go"], :, pair_cols]
            q_pair = pool[SLOT["q"], :, pair_cols]
            grads_v, grads_k = [], []
            for hh in range(2):
                head = 2 * p + hh
                rows = pl.ds(pl.multiple_of(start + hh * size, size), size)
                right = jnp.concatenate(
                    head_rows(hh == 0, pool[SLOT["q_t"], rows, :], slots) + [bias[head], pad],
                    axis=0,
                )
                prob = jnp.exp2(dot(left, right) - lse[head])
                right = jnp.concatenate(
                    head_rows(hh == 0, pool[SLOT["got"], rows, :], slots), axis=0
                )
                grad_prob = dot(v_pair, right)
                grad_score = (prob * (grad_prob - delta[head])).astype(bf16)
                grads_v.append(dot(prob.astype(bf16), go_pair))
                grads_k.append(dot(grad_score, q_pair))
                key_rows = jnp.concatenate(
                    [pool[SLOT["k_t"], rows, span], feat_t[:, span]], axis=0
                )
                found = dot(key_rows, grad_score)
                at = pl.ds(pl.multiple_of(head * stride, 8), stride)
                if part == 0:
                    dq_acc[at, :] = found
                else:
                    dq_acc[at, :] = dq_acc[at, :] + found
            pool[SLOT["dv"], span, pair_cols] = jnp.where(lane < size, *grads_v).astype(bf16)
            pool[SLOT["dk"], span, pair_cols] = (jnp.where(lane < size, *grads_k) * LN2).astype(bf16)
            return carry

        lax.fori_loop(0, heads // 2, pair, 0)
        if part == 0:
            load("wk").wait()
            load("wv").wait()
        pool[SLOT["send"], span, :] = (
            dot(pool[SLOT["dk"], span, :], pool[SLOT["wk"]], "nt")
            + dot(pool[SLOT["dv"], span, :], pool[SLOT["wv"]], "nt")
        ).astype(bf16)
        remote(
            slot("send").at[span, :], slot("back").at[span, :], xsem.at[part], xrem.at[part], x_peer
        ).start()
        if part == 0:
            after_y_down(1)
            after_y_rest(1)
        elif part == 1:
            after_y_down(2)
            after_y_rest(2)

    load("far").wait()
    pool[SLOT["sk"]] = dot(pool[SLOT["far"]], pool[SLOT["dk"]], "tn").astype(bf16)
    core_rest(5, SLOT["sk"]).start()
    pool[SLOT["sv"]] = dot(pool[SLOT["far"]], pool[SLOT["dv"]], "tn").astype(bf16)
    core_rest(6, SLOT["sv"]).start()
    after_core_rest(5, SLOT["sk"])
    for head in range(heads):
        pool[SLOT["dq_t"], head * size : (head + 1) * size, :] = (
            dq_acc[head * stride : head * stride + size, :] * size**-0.5
        ).astype(bf16)
    pool[SLOT["dq"]] = pool[SLOT["dq_t"]].T
    load("normed").wait()
    load("wq").wait()
    pool[SLOT["sq"]] = dot(pool[SLOT["normed"]], pool[SLOT["dq"]], "tn").astype(bf16)
    core_rest(7, SLOT["sq"]).start()
    after_core_rest(6, SLOT["sv"])
    wide[1] = dot(pool[SLOT["dq"]], pool[SLOT["wq"]], "nt")
    after_core_rest(7, SLOT["sq"])
    after_y_down(3)
    after_y_rest(3)

    def table_rows(head, carry):
        at = pl.multiple_of(head * stride + size, 8)
        cell = dq_acc[pl.ds(at, 2 * GRID), :]
        for bucket in range(7):
            kept = jnp.where(offsets[...] == bucket, cell, 0.0)
            cells[pl.ds(bucket * heads + head, 1), :] = jnp.sum(kept[:GRID], axis=0, keepdims=True)
            cells[pl.ds((7 + bucket) * heads + head, 1), :] = jnp.sum(
                kept[GRID:], axis=0, keepdims=True
            )
        return carry

    lax.fori_loop(0, heads, table_rows, 0)
    table_o[...] = lax.dot_general(
        jnp.ones((8, width), f32),
        cells[...],
        (((1,), (1,)), ((), ())),
        preferred_element_type=f32,
        precision=lax.Precision.HIGHEST,
    )

    after_y_rest(4)
    for part in range(3):
        span = spans[part]
        remote(
            slot("send").at[span, :], slot("back").at[span, :], xsem.at[part], xrem.at[part], x_peer
        ).wait()
    for span in spans:
        grad_one = wide[1, span, :] + pool[SLOT["back"], span, :].astype(f32)
        plain, inverse = plain_norm(wide[0, span, :])
        sums[0:1, :] += jnp.sum(grad_one * plain, axis=0, keepdims=True)
        sums[2:3, :] += jnp.sum(grad_one, axis=0, keepdims=True)
        wide[1, span, :] = wide[2, span, :] + norm_backward(
            grad_one, plain, inverse, gains[0:1, :]
        )
    pltpu.make_async_copy(wide.at[1], grad_o, out_sem.at[1]).start()

    def small_copies(i, peer):
        return (
            remote(sums, sums_in.at[i], asem.at[i], arem.at[i], peer),
            remote(table_o, table_in.at[i], bsem.at[i], brem.at[i], peer),
        )

    def small_start(i, peer):
        for copy in small_copies(i, peer):
            copy.start()

    def small_end(i, peer):
        for copy in small_copies(i, peer):
            copy.wait()
        sums[...] = sums[...] + sums_in[i]
        table_o[...] = table_o[...] + table_in[i]

    def hop_copy(i):
        return remote(hop.at[i], hop_in.at[i], hsem.at[i], hrem.at[i], x_peer)

    small_start(0, core_peer)
    after_y_rest(5)
    small_end(0, core_peer)
    small_start(1, y_peer)
    end_down()
    for q in range(4):
        up_o[:, q * width : (q + 1) * width] = end_rest(q)
    small_end(1, y_peer)
    small_start(2, one_peer)
    wo_o[...] = end_rest(4)
    after_y_rest(6)
    small_end(2, one_peer)
    small_start(3, two_peer)
    hop[0] = end_rest(5).astype(bf16)
    hop_copy(0).start()
    small_end(3, two_peer)
    last = remote(table_o, table_in.at[4], bsem.at[4], brem.at[4], x_peer)
    last.start()
    after_y_rest(7)
    hop[1] = end_rest(6).astype(bf16)
    hop_copy(1).start()
    last.wait()
    column = lax.broadcasted_iota(jnp.int32, table_o.shape, 1)
    table_o[...] = table_o[...] + jnp.where(column >= 168, table_in[4], 0.0)
    wq_o[...] = end_rest(7)
    gains_o[...] = sums[0:2, :]
    shifts_o[...] = sums[2:4, :]
    down_bias_o[...] = sums[4:5, :]
    for q in range(4):
        up_bias_o[:, q * width : (q + 1) * width] = sums[5 + q : 6 + q, :]
    hop_copy(0).wait()
    wk_o[...] = hop_in[0].astype(f32)
    hop_copy(1).wait()
    wv_o[...] = hop_in[1].astype(f32)
    pltpu.make_async_copy(wide.at[1], grad_o, out_sem.at[1]).wait()


def features(first, second, page):
    cell = jnp.arange(GRID, dtype=jnp.int32)
    one = first[:, None] == cell[None, :]
    two = second[:, None] == cell[None, :]
    pages = page[:, None] == jnp.arange(PAGES + 1, dtype=jnp.int32)[None, :]
    hot = jnp.concatenate([one, two, one, two, pages], axis=1).astype(bf16)
    return jnp.pad(hot, ((0, 0), (0, 128 - hot.shape[1])))


def bias_rows(rel_table, first, second, page):
    buckets = rel_table.shape[0] // 2
    radius = (buckets - 1) // 2
    cell = jnp.arange(GRID, dtype=jnp.int32)[:, None]
    offsets = [
        jnp.clip(coord[None, :] - cell, -radius, radius) + radius for coord in (first, second)
    ]
    exact = []
    for part, offset in enumerate(offsets):
        total = jnp.zeros((rel_table.shape[1],) + offset.shape, f32)
        for bucket in range(buckets):
            entry = rel_table[part * buckets + bucket][:, None, None]
            total = jnp.where((offset == bucket)[None], entry, total)
        exact.append(total * LOG2E)
    exact = jnp.concatenate(exact, axis=1)
    high = lax.reduce_precision(exact, 8, 7)
    low = exact - high
    pages = jnp.arange(PAGES + 1, dtype=jnp.int32)[:, None]
    allowed = (page[None, :] == pages) | (page[None, :] == PAGES)
    mask = jnp.where(allowed, 0.0, masked_fill)
    mask = jnp.broadcast_to(mask[None], (exact.shape[0],) + mask.shape)
    rows = jnp.concatenate([high, low, mask], axis=1).astype(bf16)
    rows = jnp.pad(rows, ((0, 0), (0, -rows.shape[1] % 16), (0, 0)))
    return rows, jnp.concatenate(offsets, axis=0)


def far_weight(weight, count):
    rows = weight.shape[0] // count
    part = lax.dynamic_slice_in_dim(weight, lax.axis_index("batch") * rows, rows, 0)
    part = lax.ppermute(part, "stream", [(0, 1), (1, 0)])
    return lax.all_gather(part, "batch", axis=0, tiled=True)


def on_device(
    inputs,
    text_pages,
    text_boxes,
    norm_gains,
    norm_shifts,
    w_query,
    w_key,
    w_value,
    w_out,
    w_up,
    up_bias,
    w_down,
    down_bias,
    box_table,
    cotangent,
):
    slots, width = inputs.shape[2:]
    heads = box_table.shape[2]
    count = lax.axis_size("batch")
    x = inputs[0, 0]
    plain, _ = plain_norm(x)
    normed = (plain * norm_gains[0, 0] + norm_shifts[0, 0]).astype(bf16)
    far = lax.ppermute(normed, "stream", [(0, 1), (1, 0)])
    far_key = far_weight(w_key[0], count)
    far_value = far_weight(w_value[0], count)

    is_text = lax.axis_index("stream") == 0
    positions = jnp.arange(slots, dtype=jnp.int32)
    cell = positions % (GRID * GRID)
    text = (text_boxes[0, 0], text_boxes[0, 1], text_pages[0])
    vision = (cell % GRID, cell // GRID, positions // (GRID * GRID))
    own = [jnp.where(is_text, a, b) for a, b in zip(text, vision)]
    other = [jnp.where(is_text, b, a) for a, b in zip(text, vision)]
    valid = jnp.where(is_text, text_pages[0] < PAGES, True).astype(f32)
    feat = features(*other)
    feat_t = feat[:, : 2 * GRID].T
    bias, offsets = bias_rows(box_table[0], *own)

    matrix = jax.ShapeDtypeStruct((slots, width), bf16)
    vmem = pl.BlockSpec(memory_space=pltpu.VMEM)
    hbm = pl.BlockSpec(memory_space=pl.ANY)
    limit = 61 * 2**20
    q, k, v, att, lse = pl.pallas_call(
        attend_kernel,
        out_shape=[matrix] * 4 + [jax.ShapeDtypeStruct((heads, 1, slots), f32)],
        in_specs=[vmem] * 8,
        out_specs=[vmem] * 5,
        scratch_shapes=[pltpu.VMEM((slots, width), bf16)] * 3,
        compiler_params=pltpu.CompilerParams(vmem_limit_bytes=limit),
        name="attend",
    )(normed, far, w_query[0], far_key, far_value, feat, bias, valid[None, :])

    part = width // 16
    wide_shape = lambda *shape: jax.ShapeDtypeStruct(shape, f32)
    dma = pltpu.SemaphoreType.DMA
    outs = pl.pallas_call(
        layer_kernel,
        out_shape=[
            wide_shape(slots, width),
            wide_shape(slots, width),
            wide_shape(4 * part, width),
            wide_shape(part, 4 * width),
            wide_shape(part, width),
            wide_shape(part, width),
            wide_shape(part, width),
            wide_shape(part, width),
            wide_shape(2, width),
            wide_shape(2, width),
            wide_shape(1, width),
            wide_shape(1, 4 * width),
            wide_shape(8, 176),
        ],
        in_specs=[hbm] * 14 + [vmem] * 11,
        out_specs=[hbm] * 2 + [vmem] * 11,
        scratch_shapes=[
            pltpu.VMEM((17, slots, width), bf16),
            pltpu.VMEM((5, slots, width), f32),
            pltpu.VMEM((heads, 1, slots), f32),
            pltpu.VMEM((176, width), f32),
            pltpu.VMEM((4, 2, 4 * part, width), bf16),
            pltpu.VMEM((8, 4, 2, part, width), bf16),
            pltpu.VMEM((4, 4 * part, width), bf16),
            pltpu.VMEM((8, 4, part, width), bf16),
            pltpu.VMEM((3, 4 * part, width), bf16),
            pltpu.VMEM((8, 3, part, width), bf16),
            pltpu.VMEM((2, part, width), bf16),
            pltpu.VMEM((2, part, width), bf16),
            pltpu.VMEM((16, width), f32),
            pltpu.VMEM((4, 16, width), f32),
            pltpu.VMEM((5, 8, 176), f32),
            dma((12,)),
            dma((2, 2)),
            dma((2,)),
            dma((12,)),
            dma((12,)),
            dma((12,)),
            dma((12,)),
            dma((9, 3)),
            dma((9, 3)),
            dma((3,)),
            dma((3,)),
            dma((2,)),
            dma((2,)),
            dma((4,)),
            dma((4,)),
            dma((5,)),
            dma((5,)),
        ],
        compiler_params=pltpu.CompilerParams(
            collective_id=0, has_side_effects=True, vmem_limit_bytes=limit
        ),
        name="layer",
    )(
        x,
        cotangent[0, 0],
        att,
        q,
        k,
        v,
        normed,
        far,
        w_query[0],
        far_key,
        far_value,
        w_out[0],
        w_up[0],
        w_down[0],
        lse,
        up_bias.reshape(4, 1, width),
        down_bias,
        norm_gains[0],
        norm_shifts[0],
        valid[:, None],
        valid[None, :],
        feat,
        feat_t,
        bias,
        offsets,
    )
    block, grad_in, down, up, out, query, key, value, gains, shifts, down_b, up_b, table = outs
    grad_table = table[0, : 14 * heads].reshape(1, 14, heads)
    sums = table[0, 14 * heads : 14 * heads + 3]
    stats = jnp.sqrt(sums[:2] / (sums[2] * width))
    return (
        block[None, None],
        grad_in[None, None],
        gains[None],
        shifts[None],
        query[None],
        key[None],
        value[None],
        out[None],
        up[None],
        up_b,
        down[None],
        down_b,
        grad_table,
        stats,
    )


def partner(block, axis, bit):
    count = lax.axis_size(axis)
    route = []
    for low in range(count):
        high = low | 1 << bit
        if high != low and high < count:
            route += [(low, high), (high, low)]
    return lax.ppermute(block, axis, route)


def norm_forward(values, gain_row, shift_row):
    center = values - jnp.mean(values, axis=-1, keepdims=True)
    inverse = lax.rsqrt(jnp.mean(center * center, axis=-1, keepdims=True) + 1e-05)
    normal_part = center * inverse
    return (normal_part * gain_row + shift_row, normal_part, inverse)


def general_norm_backward(grad_normed, normal_part, inverse, gain_row):
    scaled = grad_normed * gain_row
    first_mean = jnp.mean(scaled, axis=-1, keepdims=True)
    second_mean = jnp.mean(scaled * normal_part, axis=-1, keepdims=True)
    return inverse * (scaled - first_mean - normal_part * second_mean)


def bucket_offset(own_coord, far_coord, bucket_count):
    radius = (bucket_count - 1) // 2
    return jnp.clip(own_coord[:, None] - far_coord[None, :], -radius, radius) + radius


def bias_from(rel_table, offset):
    result = jnp.zeros((rel_table.shape[1],) + offset.shape, f32)
    for bucket in range(rel_table.shape[0]):
        result = (
            result + rel_table[bucket][:, None, None] * (offset == bucket).astype(f32)[None]
        )
    return result


def bias_grad(grad_wide, offset, bucket_count):
    return jnp.stack(
        [
            jnp.sum(grad_wide * (offset == bucket).astype(f32)[None], axis=(1, 2))
            for bucket in range(bucket_count)
        ]
    )


def project(left, right):
    return jnp.einsum("rsd,de->rse", left, right, preferred_element_type=f32)


def weight_grad(left, right):
    return jnp.einsum("rsd,rse->de", left, right, preferred_element_type=f32)


def back_project(grad_low, weight):
    return jnp.einsum("rse,de->rsd", grad_low, weight, preferred_element_type=f32)


def general_device(
    inputs,
    text_pages,
    text_boxes,
    norm_gains,
    norm_shifts,
    w_query,
    w_key,
    w_value,
    w_out,
    w_up,
    up_bias,
    w_down,
    down_bias,
    box_table,
    cotangent,
):
    slot_count = inputs.shape[2]
    model_width = inputs.shape[3]
    head_count = box_table.shape[2]
    head_size = model_width // head_count
    bucket_count = box_table.shape[1] // 2
    score_scale = head_size ** (-0.5)
    is_text = lax.axis_index("stream") == 0
    positions = jnp.arange(slot_count, dtype=jnp.int32)
    cell_index = positions % (GRID * GRID)
    vision_page = positions // (GRID * GRID)
    vision_first = cell_index % GRID
    vision_second = cell_index // GRID
    own_valid = jnp.where(is_text, text_pages < PAGES, True).astype(f32)
    gain_rows = norm_gains[0]
    shift_rows = norm_shifts[0]
    rel_table = box_table[0]
    block_in = inputs[:, 0]
    normed_one, plain_one, inverse_one = norm_forward(block_in, gain_rows[0], shift_rows[0])
    normed_low = normed_one.astype(bf16)
    query = project(normed_low, w_query[0]).astype(bf16)
    own_keys = project(normed_low, w_key[0]).astype(bf16)
    own_values = project(normed_low, w_value[0]).astype(bf16)
    far_keys, far_values = partner((own_keys, own_values), "stream", 0)

    def geometry(row_index):
        text_page = text_pages[row_index]
        own_page = jnp.where(is_text, text_page, vision_page)
        far_page = jnp.where(is_text, vision_page, text_page)
        own_first = jnp.where(is_text, text_boxes[row_index, 0], vision_first)
        far_first = jnp.where(is_text, vision_first, text_boxes[row_index, 0])
        own_second = jnp.where(is_text, text_boxes[row_index, 1], vision_second)
        far_second = jnp.where(is_text, vision_second, text_boxes[row_index, 1])
        allowed = (own_page[:, None] == far_page[None, :]) | (own_page[:, None] == PAGES)
        return (
            allowed,
            bucket_offset(own_first, far_first, bucket_count),
            bucket_offset(own_second, far_second, bucket_count),
        )

    def heads_of(matrix):
        return matrix.reshape(slot_count, head_count, head_size)

    def score_block(row_index, allowed, offset_first, offset_second):
        raw = (
            jnp.einsum(
                "ihd,jhd->hij",
                heads_of(query[row_index]),
                heads_of(far_keys[row_index]),
                preferred_element_type=f32,
            )
            * score_scale
        )
        raw = (
            raw
            + bias_from(rel_table[:bucket_count], offset_first)
            + bias_from(rel_table[bucket_count:], offset_second)
        )
        return jnp.where(allowed[None], raw, masked_fill)

    row_index = 0
    allowed, offset_first, offset_second = geometry(row_index)
    masked = score_block(row_index, allowed, offset_first, offset_second)
    top_score = jnp.max(masked, axis=-1, keepdims=True)
    exp_scores = jnp.exp(masked - top_score)
    row_total = jnp.sum(exp_scores, axis=-1, keepdims=True)
    prob_low = (exp_scores / row_total).astype(bf16)
    attended = jnp.einsum(
        "hij,jhd->ihd",
        prob_low,
        heads_of(far_values[row_index]),
        preferred_element_type=f32,
    ).reshape(slot_count, model_width)
    attended_rows = [(attended * own_valid[row_index][:, None]).astype(bf16)]
    log_totals = [top_score + jnp.log(row_total)]
    attended_low = jnp.stack(attended_rows)
    branch_one = project(attended_low, w_out[0])
    middle = block_in + branch_one
    normed_two, plain_two, inverse_two = norm_forward(middle, gain_rows[1], shift_rows[1])
    normed_two_low = normed_two.astype(bf16)
    pre_act = project(normed_two_low, w_up[0]) + up_bias[0]
    act_low = jax.nn.gelu(pre_act).astype(bf16)
    branch_two = project(act_low, w_down[0]) + down_bias[0]
    block_out = middle + branch_two
    sublayer = branch_one + branch_two
    totals = lax.psum(
        (
            jnp.sum(own_valid * jnp.sum(block_out * block_out, axis=-1)),
            jnp.sum(own_valid * jnp.sum(sublayer * sublayer, axis=-1)),
            jnp.sum(own_valid),
        ),
        ("stream", "batch"),
    )
    denominator = totals[2] * model_width
    stats = jnp.stack([jnp.sqrt(totals[0] / denominator), jnp.sqrt(totals[1] / denominator)])
    grad_out = cotangent[:, 0]
    grad_out_low = grad_out.astype(bf16)
    grad_w_down = weight_grad(act_low, grad_out_low)
    grad_down_bias = jnp.sum(grad_out_low.astype(f32), axis=(0, 1))
    grad_act = back_project(grad_out_low, w_down[0])
    gelu_back = jax.vjp(jax.nn.gelu, pre_act)[1]
    grad_pre_low = gelu_back(grad_act)[0].astype(bf16)
    grad_w_up = weight_grad(normed_two_low, grad_pre_low)
    grad_up_bias = jnp.sum(grad_pre_low.astype(f32), axis=(0, 1))
    grad_normed_two = back_project(grad_pre_low, w_up[0])
    grad_gain_two = jnp.sum(grad_normed_two * plain_two, axis=(0, 1))
    grad_shift_two = jnp.sum(grad_normed_two, axis=(0, 1))
    grad_middle = grad_out + general_norm_backward(grad_normed_two, plain_two, inverse_two, gain_rows[1])
    grad_middle_low = grad_middle.astype(bf16)
    grad_w_out = weight_grad(attended_low, grad_middle_low)
    grad_attended = back_project(grad_middle_low, w_out[0]).astype(bf16) * own_valid[
        :, :, None
    ].astype(bf16)
    query_grad_rows, key_grad_rows, value_grad_rows = ([], [], [])
    row_index = 0
    allowed, offset_first, offset_second = geometry(row_index)
    masked = score_block(row_index, allowed, offset_first, offset_second)
    prob = jnp.exp(masked - log_totals[row_index])
    grad_heads = heads_of(grad_attended[row_index])
    grad_prob = jnp.einsum(
        "ihd,jhd->hij",
        grad_heads,
        heads_of(far_values[row_index]),
        preferred_element_type=f32,
    )
    inner_sum = jnp.sum(prob * grad_prob, axis=-1, keepdims=True)
    grad_score_low = (prob * (grad_prob - inner_sum)).astype(bf16)
    grad_score_wide = grad_score_low.astype(f32)
    grad_table = jnp.concatenate(
        [
            bias_grad(grad_score_wide, offset_first, bucket_count),
            bias_grad(grad_score_wide, offset_second, bucket_count),
        ],
        axis=0,
    )
    query_grad = (
        jnp.einsum(
            "hij,jhd->ihd",
            grad_score_low,
            heads_of(far_keys[row_index]),
            preferred_element_type=f32,
        )
        * score_scale
    )
    key_grad = (
        jnp.einsum(
            "hij,ihd->jhd",
            grad_score_low,
            heads_of(query[row_index]),
            preferred_element_type=f32,
        )
        * score_scale
    )
    value_grad = jnp.einsum(
        "hij,ihd->jhd", prob.astype(bf16), grad_heads, preferred_element_type=f32
    )
    query_grad_rows.append(query_grad.reshape(slot_count, model_width).astype(bf16))
    key_grad_rows.append(key_grad.reshape(slot_count, model_width).astype(bf16))
    value_grad_rows.append(value_grad.reshape(slot_count, model_width).astype(bf16))
    grad_query_low = jnp.stack(query_grad_rows)
    own_key_grad, own_value_grad = partner(
        (jnp.stack(key_grad_rows), jnp.stack(value_grad_rows)), "stream", 0
    )
    grad_w_query = weight_grad(normed_low, grad_query_low)
    grad_w_key = weight_grad(normed_low, own_key_grad)
    grad_w_value = weight_grad(normed_low, own_value_grad)
    grad_normed_one = (
        back_project(grad_query_low, w_query[0])
        + back_project(own_key_grad, w_key[0])
        + back_project(own_value_grad, w_value[0])
    )
    grad_gain_one = jnp.sum(grad_normed_one * plain_one, axis=(0, 1))
    grad_shift_one = jnp.sum(grad_normed_one, axis=(0, 1))
    grad_inputs = grad_middle + general_norm_backward(grad_normed_one, plain_one, inverse_one, gain_rows[0])
    big_sums = (
        lax.psum_scatter(grad_w_query, "batch", scatter_dimension=0, tiled=True),
        lax.psum_scatter(grad_w_key, "batch", scatter_dimension=0, tiled=True),
        lax.psum_scatter(grad_w_value, "batch", scatter_dimension=0, tiled=True),
        lax.psum_scatter(grad_w_out, "batch", scatter_dimension=0, tiled=True),
        lax.psum_scatter(grad_w_up, "batch", scatter_dimension=0, tiled=True),
        lax.psum_scatter(grad_w_down, "batch", scatter_dimension=0, tiled=True),
    )
    small_sums = lax.psum(
        (
            jnp.stack([grad_gain_one, grad_gain_two]),
            jnp.stack([grad_shift_one, grad_shift_two]),
            grad_up_bias,
            grad_down_bias,
            grad_table,
        ),
        "batch",
    )
    return (
        block_out[:, None],
        grad_inputs[:, None],
        small_sums[0][None],
        small_sums[1][None],
        big_sums[0][None],
        big_sums[1][None],
        big_sums[2][None],
        big_sums[3][None],
        big_sums[4][None],
        small_sums[2][None],
        big_sums[5][None],
        small_sums[3][None],
        small_sums[4][None],
        stats,
    )


def solution(mesh):
    sided = lambda dims: P("stream", *([None] * (dims - 1)))
    rows = P("batch", "stream", None, None)
    shard = P("stream", "batch", None)
    placed = (
        (rows, P("batch", None), P("batch", None, None), sided(3), sided(3))
        + (sided(3),) * 5
        + (sided(2), sided(3), sided(2), sided(3), rows)
    )
    fits = mesh.shape["batch"] == 16 and mesh.shape["stream"] == 2
    return jax.shard_map(
        on_device if fits else general_device,
        mesh=mesh,
        in_specs=placed,
        out_specs=(
            (rows, rows, sided(3), sided(3))
            + (shard,) * 5
            + (sided(2), shard, sided(2), sided(3), P())
        ),
        check_vma=False,
    )
```

time: 721 us -> 274 us (0.38)
  matrix products: 204 us -> 0 us
  waiting for transfers between devices: 268 us -> 66.3 us
  Pallas kernels: 0 us -> 149 us
  blocking collectives: 100 us -> 0 us
  other arithmetic: 89.7 us -> 11 us
  local copies, waits for them, and re-layouts: 31.1 us -> 22.6 us
    dot_general x24 -> x0, matrix products: 204 us -> none  [the longest x1 44.4 us: score_block(): jnp.einsum('ihd,jhd->hij', heads_of(query[row_index]), heads_of(far_keys[...]
    reduce_scatter x6 -> x0, waiting for transfers between devices: 200 us -> none  [the longest x1 116 us: on_device(): lax.psum_scatter(grad_w_up, 'batch', scatter_dimension=0, tiled=True)]
    pallas_call x0 -> x2, Pallas kernels: none -> 149 us  [the longest x1 130 us: on_device(): pl.pallas_call(layer_kernel, out_shape=[wide_shape(slots, width), wide_sh...]
    psum x2 -> x0, blocking collectives: 100 us -> none  [the longest x1 59.6 us: on_device(): lax.psum((jnp.stack([grad_gain_one, grad_gain_two]), jnp.stack([grad_shif...]
    reduce_sum x7 -> x2, other arithmetic: 64.4 us -> 2.24 us  [the longest x1 1.85 us: plain_norm(): center = values - jnp.mean(values, axis=-1, keepdims=True)]
    ppermute x4 -> x3, waiting for transfers between devices: 68 us -> 16.3 us  [the longest x1 16.3 us: on_device(): far = lax.ppermute(normed, 'stream', [(0, 1), (1, 0)])]
    all_gather x0 -> x2, waiting for transfers between devices: none -> 50 us  [far_weight(): return lax.all_gather(part, 'batch', axis=0, tiled=True)]
    convert_element_type x5 -> x2, other arithmetic: 16 us -> 2.16 us  [the longest x1 2.15 us: on_device(): normed = (plain * norm_gains[0, 0] + norm_shifts[0, 0]).astype(bf16)]
  transfers between devices with their start and end apart: 10 -> 5, of which waited for: 5 -> 3; matrix products, arithmetic and copies ran while one was open for 34% -> 6% of each run, Pallas kernels for 0% -> 0%
where the time goes in v2:
time: 274 us; the launch traced here: 269 us
  Pallas kernels  149 us (54%)
  waiting for transfers between devices  66.3 us (24%)
  local copies, waits for them, and re-layouts  22.6 us (8%)
  between operations  15.5 us (6%)
  other arithmetic  11 us (4%)
  starting transfers between devices  5.04 us (2%)
    pallas_call x1, Pallas kernels, on_device(): pl.pallas_call(layer_kernel, out_shape=[wide_shape(slots, width), wide_sh...  130 us
    all_gather x2, waiting for transfers between devices, far_weight(): return lax.all_gather(part, 'batch', axis=0, tiled=True)  50 us
    pallas_call x1, Pallas kernels, on_device(): pl.pallas_call(attend_kernel, out_shape=[matrix] * 4 + [jax.ShapeDtypeStr...  18.3 us
    ppermute x1, waiting for transfers between devices, on_device(): far = lax.ppermute(normed, 'stream', [(0, 1), (1, 0)])  16.3 us
    unnamed x62, local copies, waits for them, and re-layouts  13.6 us
  transfers between devices with their start and end apart: 5, of which 3 were waited for; matrix products, arithmetic and copies ran while one was open for 6% of the time, Pallas kernels for 0%

profile of v2, /device:TPU:0, one launch (start us, length us, event | category | flops | bytes accessed | tf_op | source)
XLA Modules:
  0.0 269.1 jit_solution(16664812476943471517)
XLA Ops:
  7.3 1.2 copy-done
  8.5 0.6 dynamic-slice_bitcast_fusion
  9.1 2.9 %collective-permute-start.2 = (bf16[48,768]{1,0:T(8,128)(2,1)}, bf16[48,768]{1,0:T(8,128)(2,1)}, u32[]{:S(2)}, u32[]{:S(2)}) collective-permute-start(bf16[48,768]{1,0:T(8,128)(2,1)} %dynamic-slice_bitcast_fusion), channel_id=1, source_target_pairs={{0,16},{16,0},{1,17},{17,1},{2,18},{18,2},{3,19},{19,3},{4,20},{20... | collective-permute-start | bytes 221192 | tf_op jit(solution)/shard_map/ppermute | solution.py:548
  12.0 1.5 dynamic-slice_bitcast_fusion.1
  13.6 1.8 reduce_sum.18
  15.5 0.4 multiply_reduce_fusion
  15.8 0.6 add_rsqrt_fusion
  16.5 0.6 slice_reduce_fusion.16
  17.1 0.0 all-gather.3.cloned.1.call-start
  17.2 2.2 add_convert_fusion.normed
  19.3 2.0 collective-permute-start
  21.3 0.8 slice_reduce_fusion.14
  22.3 0.7 compare_reduce_fusion
  23.0 0.7 reduce.5
  23.8 1.1 slice_reduce_fusion.13
  24.8 0.1 fusion.12
  24.9 0.1 fusion.19
  25.0 0.5 select_multiply_fusion.1
  25.5 0.2 copy.36
  25.7 0.9 copy.33.valid_col
  26.7 0.7 pad.8.clone.feat
  27.4 0.6 pad_add_fusion.offsets
  28.1 0.5 select_multiply_fusion
  28.5 0.2 reduce-precision_convert_fusion
  28.8 1.2 fusion.4.bias
  30.0 0.6 slice_bitcast_fusion.feat_t
  30.6 16.3 %collective-permute-done.far = bf16[768,768]{1,0:T(8,128)(2,1)S(1)} collective-permute-done((bf16[768,768]{1,0:T(8,128)(2,1)}, bf16[768,768]{1,0:T(8,128)(2,1)S(1)}, u32[]{:S(2)}, u32[]{:S(2)}) %collective-permute-start) | collective-permute-done | bytes 1179680 | tf_op jit(solution)/shard_map/ppermute | solution.py:575
  47.0 10.4 %all-gather.5.cloned.1.call-done.wv = bf16[768,768]{1,0:T(8,128)(2,1)} async-done(((bf16[48,768]{1,0:T(8,128)(2,1)}), bf16[768,768]{1,0:T(8,128)(2,1)}) %all-gather.5.cloned.1.call-update) | async-done | bytes 1179664 | tf_op jit(solution)/shard_map/all_gather | solution.py:549
  57.4 39.6 %all-gather.3.cloned.1.call-done.wk = bf16[768,768]{1,0:T(8,128)(2,1)} async-done(((bf16[48,768]{1,0:T(8,128)(2,1)}), bf16[768,768]{1,0:T(8,128)(2,1)}) %all-gather.3.cloned.1.call-update) | async-done | bytes 1179664 | tf_op jit(solution)/shard_map/all_gather | solution.py:549
  97.0 18.3 %attend.1 = (bf16[768,768]{1,0:T(8,128)(2,1)}, bf16[768,768]{1,0:T(8,128)(2,1)}, bf16[768,768]{1,0:T(8,128)(2,1)}, bf16[768,768]{1,0:T(8,128)(2,1)}, f32[12,1,768]{2,1,0:T(1,128)}) custom-call(bf16[768,768]{1,0:T(8,128)(2,1)} %add_convert_fusion.normed, bf16[768,768]{1,0:T(8,128)(2,1)} %copy-done.2, bf16[768,768]{1,0:T(8,128)(2,1)} %bitcast.34, ...), custom_call_target="tpu_custom_call" | custom-call | tf_op jit(solution)/shard_map/attend/pallas_call | solution.py:595
  115.3 130.3 %layer.1 = (f32[768,768]{1,0:T(8,128)}, f32[768,768]{1,0:T(8,128)}, f32[192,768]{1,0:T(8,128)}, f32[48,3072]{1,0:T(8,128)}, f32[48,768]{1,0:T(8,128)}, /*index=5...) custom-call(f32[768,768]{1,0:T(8,128)} %bitcast.31, ...), custom_call_target="tpu_custom_call" | custom-call | tf_op jit(solution)/shard_map/layer/pallas_call | solution.py:608
  245.6 1.3 slice.107
  246.9 0.7 slice_reduce_fusion.18
  248.2 1.3 sqrt_bitcast_fusion
  249.5 0.1 reshape_squeeze.3
  249.6 0.7 copy.35
  250.3 3.4 %copy.53 = f32[1,1,768,768]{3,2,1,0:T(8,128)} copy(f32[1,1,768,768]{3,2,1,0:T(8,128)} %bitcast.37) | data formatting | bytes 4718592
  253.7 1.4 copy.54
  255.1 0.6 copy.55
  255.7 0.6 copy.56
  256.3 0.7 copy.57
  257.0 0.7 copy.58
  257.6 0.7 copy.59
  258.3 0.7 copy.60
  259.0 0.8 copy.61
  259.8 0.6 copy.62
  260.4 0.8 copy.63
  261.2 0.6 copy.64
  (67 shorter events, 0.4 us)
Async XLA Ops:
  7.2 1.3 copy-start
  7.2 8.3 %copy-start.1 = (f32[1,1,768,768]{3,2,1,0:T(8,128)S(1)}, f32[1,1,768,768]{3,2,1,0:T(8,128)}, u32[]{:S(2)}) copy-start(f32[1,1,768,768]{3,2,1,0:T(8,128)} %param.15) | copy-start | bytes 7077892
  7.2 50.2 %all-gather.5.cloned.1.call-start = ((), (), s32[]{:S(2)}) async-start(), calls=%async_computation.1 | async-start | bytes 1253376 | tf_op jit(solution)/shard_map/all_gather | solution.py:549
  9.1 8.0 %collective-permute-start.2 = (bf16[48,768]{1,0:T(8,128)(2,1)}, bf16[48,768]{1,0:T(8,128)(2,1)}, u32[]{:S(2)}, u32[]{:S(2)}) collective-permute-start(bf16[48,768]{1,0:T(8,128)(2,1)} %dynamic-slice_bitcast_fusion), channel_id=1, source_target_pairs={{0,16},{16,0},{1,17},{17,1},{2,18},{18,2},{3,19},{19,3},{4,20},{20... | collective-permute-start | bytes 221192 | tf_op jit(solution)/shard_map/ppermute | solution.py:548
  13.6 10.2 %collective-permute-start.1 = (bf16[48,768]{1,0:T(8,128)(2,1)}, bf16[48,768]{1,0:T(8,128)(2,1)}, u32[]{:S(2)}, u32[]{:S(2)}) collective-permute-start(bf16[48,768]{1,0:T(8,128)(2,1)} %dynamic-slice_bitcast_fusion.1), channel_id=1, source_target_pairs={{0,16},{16,0},{1,17},{17,1},{2,18},{18,2},{3,19},{19,3},{4,20},{20... | collective-permute-start | bytes 221192 | tf_op jit(solution)/shard_map/ppermute | solution.py:548
  15.4 1.0 copy-start.12
  15.4 1.0 copy-start.13
  17.1 79.9 %all-gather.3.cloned.1.call-start = ((), (), s32[]{:S(2)}) async-start(), calls=%async_computation | async-start | bytes 1253376 | tf_op jit(solution)/shard_map/all_gather | solution.py:549
  17.2 6.6 %copy-start.4 = (f32[1,14,12]{1,0,2:T(1,128)S(1)}, f32[1,14,12]{1,0,2:T(1,128)}, u32[]{:S(2)}) copy-start(f32[1,14,12]{1,0,2:T(1,128)} %param.28) | copy-start | bytes 2020
  19.3 27.6 %collective-permute-start = (bf16[768,768]{1,0:T(8,128)(2,1)}, bf16[768,768]{1,0:T(8,128)(2,1)S(1)}, u32[]{:S(2)}, u32[]{:S(2)}) collective-permute-start(bf16[768,768]{1,0:T(8,128)(2,1)} %add_convert_fusion.normed), channel_id=1, source_target_pairs={{0,16},{16,0},{1,17},{17,1},{2,18},{18,2},{3,19},{19,3},{4,20},{20... | collective-permute-start | bytes 3538952 | tf_op jit(solution)/shard_map/ppermute | solution.py:575
  23.0 5.5 %copy-start.11 = (f32[1,768]{1,0:T(1,128)}, f32[1,768]{1,0:T(1,128)S(1)}, u32[]{:S(2)}) copy-start(f32[1,768]{1,0:T(1,128)S(1)} %get-tuple-element.116.valid_row) | copy-start | bytes 9220
  24.8 3.2 %copy-start.18 = (f32[12]{0:T(128)S(1)}, f32[12]{0:T(128)}, u32[]{:S(2)}) copy-start(f32[12]{0:T(128)} %get-tuple-element.80) | copy-start | bytes 148
  24.8 3.2 %copy-start.19 = (f32[12]{0:T(128)S(1)}, f32[12]{0:T(128)}, u32[]{:S(2)}) copy-start(f32[12]{0:T(128)} %get-tuple-element.81) | copy-start | bytes 148
  24.9 3.1 %copy-start.20 = (f32[12]{0:T(128)S(1)}, f32[12]{0:T(128)}, u32[]{:S(2)}) copy-start(f32[12]{0:T(128)} %get-tuple-element.82) | copy-start | bytes 148
  25.0 3.1 %copy-start.21 = (f32[12]{0:T(128)S(1)}, f32[12]{0:T(128)}, u32[]{:S(2)}) copy-start(f32[12]{0:T(128)} %get-tuple-element.83) | copy-start | bytes 148
  25.5 2.6 copy-start.22
  25.5 2.6 copy-start.23
  47.0 50.0 %copy-start.2 = (bf16[768,768]{1,0:T(8,128)(2,1)}, bf16[768,768]{1,0:T(8,128)(2,1)S(1)}, u32[]{:S(2)}) copy-start(bf16[768,768]{1,0:T(8,128)(2,1)S(1)} %collective-permute-done.far) | copy-start | bytes 3538948
  250.3 3.4 %copy-start.3 = (f32[768,768]{1,0:T(8,128)S(1)}, f32[768,768]{1,0:T(8,128)}, u32[]{:S(2)}) copy-start(f32[768,768]{1,0:T(8,128)} %get-tuple-element.38) | copy-start | bytes 7077892
  253.6 1.4 copy-start.16
  253.6 2.1 copy-start.15
  253.6 2.6 copy-start.10
  253.7 3.3 %copy-start.9 = (f32[48,768]{1,0:T(8,128)S(1)}, f32[48,768]{1,0:T(8,128)}, u32[]{:S(2)}) copy-start(f32[48,768]{1,0:T(8,128)} %get-tuple-element.42) | copy-start | bytes 442372
  253.7 4.0 %copy-start.8 = (f32[48,768]{1,0:T(8,128)S(1)}, f32[48,768]{1,0:T(8,128)}, u32[]{:S(2)}) copy-start(f32[48,768]{1,0:T(8,128)} %get-tuple-element.43) | copy-start | bytes 442372
  253.7 4.6 %copy-start.7 = (f32[48,768]{1,0:T(8,128)S(1)}, f32[48,768]{1,0:T(8,128)}, u32[]{:S(2)}) copy-start(f32[48,768]{1,0:T(8,128)} %get-tuple-element.44) | copy-start | bytes 442372
  255.1 3.9 %copy-start.6 = (f32[48,3072]{1,0:T(8,128)S(1)}, f32[48,3072]{1,0:T(8,128)}, u32[]{:S(2)}) copy-start(f32[48,3072]{1,0:T(8,128)} %get-tuple-element.45) | copy-start | bytes 1769476
  255.1 4.7 %copy-start.14 = (f32[1,3072]{1,0:T(1,128)S(1)}, f32[1,3072]{1,0:T(1,128)}, u32[]{:S(2)}) copy-start(f32[1,3072]{1,0:T(1,128)} %get-tuple-element.144) | copy-start | bytes 36868
  255.1 5.3 %copy-start.5 = (f32[192,768]{1,0:T(8,128)S(1)}, f32[192,768]{1,0:T(8,128)}, u32[]{:S(2)}) copy-start(f32[192,768]{1,0:T(8,128)} %get-tuple-element.47) | copy-start | bytes 1769476
  257.6 3.6 %copy-start.17 = (f32[1,768]{1,0:T(1,128)S(1)}, f32[1,768]{1,0:T(1,128)}, u32[]{:S(2)}) copy-start(f32[1,768]{1,0:T(1,128)} %get-tuple-element.146) | copy-start | bytes 9220
Sparse Core Ops, SparseCore 0:
  17.2 40.0 all-gather.4
  59.6 37.2 all-gather.2

commit v3 on v0

v3 whole, which is shorter than its diff:
```python
import jax
import jax.numpy as jnp
from jax import lax
from jax.experimental import pallas as pl
from jax.experimental.pallas import tpu as pltpu
from jax.sharding import PartitionSpec as P

GRID = 16
PAGES = 3
MESH = pl.DeviceIdType.MESH
LOG2E = 1.4426950408889634
LN2 = 0.6931471805599453
TOGETHER = 2
GELU_IN = 0.7978845608028654
GELU_CUBE = 0.044715
masked_fill = -1e30
f32 = jnp.float32
bf16 = jnp.bfloat16


def dot(left, right, form="nn"):
    dims = {"nn": (1, 0), "nt": (1, 1), "tn": (0, 0)}[form]
    return lax.dot_general(
        left, right, (((dims[0],), (dims[1],)), ((), ())), preferred_element_type=f32
    )


def stack(parts):
    return jnp.concatenate(parts, axis=0)


def plain_norm(values):
    center = values - jnp.mean(values, axis=-1, keepdims=True)
    inverse = lax.rsqrt(jnp.mean(center * center, axis=-1, keepdims=True) + 1e-05)
    return center * inverse, inverse


def norm_backward(grad_normed, plain, inverse, gain_row):
    scaled = grad_normed * gain_row
    first_mean = jnp.mean(scaled, axis=-1, keepdims=True)
    second_mean = jnp.mean(scaled * plain, axis=-1, keepdims=True)
    return inverse * (scaled - first_mean - plain * second_mean)


NAMES = (
    "ft", "wk", "wv", "back", "q_t", "k_t", "v_t", "att", "wo", "n2", "g2",
    "wu0", "wu1", "wd0", "wd1", "sd0", "sd1", "sr0", "sr1", "act", "gp",
)
SLOT = {name: i for i, name in enumerate(NAMES)}
for name, place in dict(
    nt="n2", wq="g2", gm="n2", go="g2", dq="wu0", dk="wu1", dv="wd0", send="wd1",
    so="sd0", sk="sd1", sv="sr0", sq="sr1", nt_again="act", wq_again="gp",
).items():
    SLOT[name] = SLOT[place]


def layer_kernel(
    x, cot, wq, wk, wv, wo, wup, wdn,
    up_bias, down_bias, gains, shifts, pages, boxes, rel_table,
    block_o, grad_o, nt_o, down_o, up_o, wo_o, wq_o, hop_o, sums_o, late_o, table_o,
    pool, wide, bias, lse, delta, page_low, page_col, cells,
    cd, cr, yd, yr, zd, zr, hop, hop_in, sums_in, late_in, table_in, table_far,
    in_sem, w_sem, out_sem, csem, crem, ysem, yrem, zsem, zrem, xsem, xrem, hsem, hrem,
    asem, arem, bsem, brem, lsem, lrem, fsem, frem, gxs, gxr, gzs, gzr, gys, gyr, gcs, gcr,
):
    slots, width = x.shape
    heads = lse.shape[0]
    size = width // heads
    third = slots // 3
    spans = [pl.ds(part * third, third) for part in range(3)]
    thirds = [slice(part * third, (part + 1) * third) for part in range(3)]
    part_rows = width // 16
    st = lax.axis_index("stream")
    me = lax.axis_index("batch")
    c = lax.rem(me, 2)
    y = lax.rem(lax.div(me, 2), 2)
    z = lax.div(me, 4)
    place = lax.rem(me, 4)
    core_peer = (st, me + 1 - 2 * c)
    y_peer = (st, me + 2 - 4 * y)
    z_at = [lax.rem(z + i, 4) for i in range(4)]
    z_peers = [(st, z_at[i] * 4 + place) for i in range(4)]
    place_at = [lax.rem(place + i, 4) for i in range(4)]
    place_peers = [(st, z * 4 + place_at[i]) for i in range(4)]
    x_peer = (1 - st, me)

    def slot(name):
        return pool.at[SLOT[name]]

    def remote(source, target, send, recv, peer):
        return pltpu.make_async_remote_copy(
            source, target, send, recv, device_id=peer, device_id_type=MESH
        )

    singles = dict(
        x=(x, wide.at[0]), cot=(cot, wide.at[1]), wo=(wo, slot("wo")), wq=(wq, slot("wq")),
        x_again=(x, wide.at[3]), wq_again=(wq, slot("wq_again")), nt_again=(nt_o, slot("nt_again")),
    )
    load_at = {name: i for i, name in enumerate(singles)}

    def load(name):
        return pltpu.make_async_copy(*singles[name], in_sem.at[load_at[name]])

    def chunk_of(t):
        return lax.rem(z + t + 1, 4)

    def chunk_loads(t):
        at = pl.multiple_of(chunk_of(t) * width, width)
        two = lax.rem(t, 2)
        return (
            pltpu.make_async_copy(
                wup.at[:, pl.ds(at, width)], pool.at[SLOT["wu0"] + two], w_sem.at[two, 0]
            ),
            pltpu.make_async_copy(
                wdn.at[pl.ds(at, width), :], pool.at[SLOT["wd0"] + two], w_sem.at[two, 1]
            ),
        )

    load("x").start()
    load("wq").start()
    load("cot").start()
    load("wo").start()
    for copy in chunk_loads(0):
        copy.start()

    barrier = pltpu.get_barrier_semaphore()
    peers = place_peers[1:] + z_peers[1:] + [x_peer]
    for peer in peers:
        pl.semaphore_signal(barrier, inc=1, device_id=peer, device_id_type=MESH)
    pl.semaphore_wait(barrier, len(peers))

    def slices(i):
        return slot(("wk", "wv")[i]).reshape(4, 2, 2, part_rows, width)

    def gather_x(i):
        source = (wk, wv)[i].at[pl.ds(pl.multiple_of(me * part_rows, 16), part_rows), :]
        return remote(source, slices(i).at[z, y, c], gxs.at[i], gxr.at[i], x_peer)

    def gather_z(i, k):
        own = slices(i).at[z, y, c]
        return remote(own, own, gzs.at[i, k - 1], gzr.at[i, k - 1], z_peers[k])

    def gather_z_here(i, k):
        found = slices(i).at[lax.rem(z + 4 - k, 4), y, c]
        return remote(found, found, gzs.at[i, k - 1], gzr.at[i, k - 1], z_peers[k])

    def gather_y(i, mine=True):
        held = slices(i).at[:, y if mine else 1 - y, c]
        return remote(held, held, gys.at[i], gyr.at[i], y_peer)

    def gather_core(i, mine=True):
        held = slices(i).at[:, :, c if mine else 1 - c]
        return remote(held, held, gcs.at[i], gcr.at[i], core_peer)

    gather_x(0).start()
    gather_x(1).start()

    def far_rows(part):
        return remote(
            slot("nt").at[:, thirds[part]],
            slot("ft").at[:, thirds[part]],
            xsem.at[part],
            xrem.at[part],
            x_peer,
        )

    load("x").wait()
    for part, span in enumerate(spans):
        plain, inverse = plain_norm(wide[0, span, :])
        low = (plain * gains[0:1, :] + shifts[0:1, :]).astype(bf16)
        pool[SLOT["nt"], :, thirds[part]] = low.T
        far_rows(part).start()
    pltpu.make_async_copy(slot("nt"), nt_o, out_sem.at[2]).start()

    page_row = pages[...].astype(f32)
    side = st.astype(f32)
    valid_row = jnp.maximum(side, jnp.where(page_row < PAGES - 0.5, 1.0, 0.0))
    page_rows = [jnp.where(page_row == p, 1.0, 0.0) for p in range(PAGES)]
    for p in range(PAGES):
        page_low[p] = jnp.broadcast_to(page_rows[p], (size, slots)).astype(bf16)
    page_col[...] = jnp.broadcast_to(page_row, (128, slots)).T
    cell = lax.broadcasted_iota(jnp.int32, (GRID, third), 0)
    spot = lax.broadcasted_iota(jnp.int32, (GRID, third), 1)
    spot_first = jnp.where(lax.rem(spot, GRID) == cell, 1.0, 0.0)
    spot_second = jnp.where(lax.div(spot, GRID) == cell, 1.0, 0.0)
    spot_once = stack([spot_first, spot_second]).astype(bf16)
    spot_twice = stack([spot_once, spot_once])
    buckets = rel_table.shape[0] // 2
    radius = (buckets - 1) // 2
    toward = 1 - 2 * st
    cell = lax.broadcasted_iota(jnp.int32, (GRID, slots), 0)
    offsets = [
        jnp.clip(toward * (boxes[axis : axis + 1, :] - cell), -radius, radius) + radius
        for axis in range(2)
    ]

    def bias_rows(head, carry):
        exact = []
        for axis in range(2):
            total = jnp.zeros((GRID, slots), f32)
            for bucket in range(buckets):
                total = jnp.where(
                    offsets[axis] == bucket, rel_table[axis * buckets + bucket, head], total
                )
            total = total * LOG2E
            if axis == 0:
                total = jnp.where(page_row > PAGES - 0.5, masked_fill, total)
            exact.append(total)
        exact = stack(exact)
        high = exact.astype(bf16)
        bias[head, : 2 * GRID, :] = high
        bias[head, 2 * GRID :, :] = (exact - high.astype(f32)).astype(bf16)
        return carry

    lax.fori_loop(0, heads, bias_rows, 0)

    load("wq").wait()
    pool[SLOT["q_t"]] = (dot(pool[SLOT["wq"]], pool[SLOT["nt"]], "tn") * (LOG2E * size**-0.5)).astype(
        bf16
    )
    sums_o[...] = jnp.zeros_like(sums_o)
    late_o[...] = jnp.zeros_like(late_o)
    load("cot").wait()
    for i in range(2):
        gather_x(i).wait()
        for k in (1, 2, 3):
            gather_z(i, k).start()
    for i in range(2):
        for k in (1, 2, 3):
            gather_z(i, k).wait_send()
            gather_z_here(i, k).wait_recv()
        gather_y(i).start()
    for i in range(2):
        gather_y(i).wait_send()
        gather_y(i, False).wait_recv()
        gather_core(i).start()
    for i in range(2):
        gather_core(i).wait_send()
        gather_core(i, False).wait_recv()
    for part in range(3):
        far_rows(part).wait()
        cols = thirds[part]
        pool[SLOT["k_t"], :, cols] = dot(pool[SLOT["wk"]], pool[SLOT["ft"], :, cols], "tn").astype(
            bf16
        )
        pool[SLOT["v_t"], :, cols] = dot(pool[SLOT["wv"]], pool[SLOT["ft"], :, cols], "tn").astype(
            bf16
        )

    def by_page(name, rows):
        return [pool[SLOT[name], rows, cols] for cols in thirds]

    def masked(name, rows):
        held = pool[SLOT[name], rows, :]
        return [held * page_low[p] for p in range(PAGES)]

    def fold(found):
        total = found[:size] * page_rows[0]
        for p in range(1, PAGES):
            total = total + found[p * size : (p + 1) * size] * page_rows[p]
        return total

    def column(p):
        return page_col[...] == p

    def spread(rows):
        middle, last = [jnp.concatenate([column(p)] * 2, axis=1) for p in (1, 2)]
        return jnp.where(middle, rows[1], jnp.where(last, rows[2], rows[0]))

    def rows_of(head):
        return pl.ds(pl.multiple_of(head * size, size), size)

    def in_pairs(step):
        def several(i, carry):
            for j in range(TOGETHER):
                step(TOGETHER * i + j, carry)
            return carry

        lax.fori_loop(0, heads // TOGETHER, several, 0)

    def text_forward(head, carry):
        rows = rows_of(head)
        scores = dot(
            stack(by_page("k_t", rows) + [spot_twice]),
            stack(masked("q_t", rows) + [bias[head]]),
            "tn",
        )
        top = jnp.max(scores, axis=0, keepdims=True)
        weight = jnp.exp2(scores - top).astype(bf16)
        found = dot(stack(by_page("v_t", rows) + [jnp.ones((16, third), bf16)]), weight)
        total = found[PAGES * size : PAGES * size + 1]
        pool[SLOT["att"], rows, :] = (fold(found) * (valid_row / total)).astype(bf16)
        lse[head] = top + jnp.log2(total)
        return carry

    def vision_forward(head, carry):
        rows = rows_of(head)
        scores = dot(
            stack(masked("k_t", rows) + [bias[head]]),
            stack(by_page("q_t", rows) + [spot_twice]),
            "tn",
        )
        tops = []
        for p in range(PAGES):
            inside = jnp.concatenate([column(p)] * 2, axis=1)
            tops.append(
                jnp.max(jnp.where(inside, scores, 2.0 * masked_fill), axis=0, keepdims=True)
            )
        weight = jnp.exp2(scores - spread(tops)).astype(bf16)
        counts = [page_low[p, :1, :] for p in range(PAGES)]
        counts = stack(counts + [jnp.zeros((16 - PAGES, slots), bf16)])
        found = dot(stack(masked("v_t", rows) + [counts]), weight)
        for p, cols in enumerate(thirds):
            total = found[PAGES * size + p : PAGES * size + p + 1]
            pool[SLOT["att"], rows, cols] = (found[p * size : (p + 1) * size] / total).astype(bf16)
            lse[head, :, cols] = tops[p] + jnp.log2(total)
        return carry

    @pl.when(st == 0)
    def _():
        in_pairs(text_forward)

    @pl.when(st == 1)
    def _():
        in_pairs(vision_forward)

    def down_view(at):
        return pool.at[at].reshape(2, 2, width // 4, width)

    def rest_view(at):
        return pool.at[at].reshape(4, 2, 2, part_rows, width)

    def core_down(t):
        at = SLOT["sd0"] + lax.rem(t, 2)
        return remote(down_view(at).at[:, 1 - c], cd.at[t], csem.at[t], crem.at[t], core_peer)

    def core_rest(p, at):
        return remote(
            rest_view(at).at[:, :, 1 - c], cr.at[p], csem.at[4 + p], crem.at[4 + p], core_peer
        )

    def y_down(t):
        return remote(cd.at[t, 1 - y], yd.at[t], ysem.at[t], yrem.at[t], y_peer)

    def y_rest(p):
        return remote(cr.at[p, :, 1 - y], yr.at[p], ysem.at[4 + p], yrem.at[4 + p], y_peer)

    def z_peer_of(t):
        return (st, chunk_of(t) * 4 + place)

    def z_down(t):
        return remote(yd.at[t], zd.at[t], zsem.at[0, t], zrem.at[0, t], z_peer_of(t))

    def z_rest(p, i):
        q = chunk_of(p) if p < 4 else p
        return remote(
            yr.at[p, z_at[i]], zr.at[q, i - 1], zsem.at[1 + p, i - 1], zrem.at[1 + q, i - 1], z_peers[i]
        )

    def z_here(q, i):
        return remote(
            yr.at[q, z_at[i]], zr.at[q, i - 1], zsem.at[1 + q, i - 1], zrem.at[1 + q, i - 1], z_peers[i]
        )

    def add_low(left, right):
        return (left.astype(f32) + right.astype(f32)).astype(bf16)

    def after_core_down(t):
        core_down(t).wait()
        cd[t] = add_low(cd[t], down_view(SLOT["sd0"] + lax.rem(t, 2))[:, c])
        y_down(t).start()

    def after_core_rest(p, at):
        core_rest(p, at).wait()
        cr[p] = add_low(cr[p], rest_view(at)[:, :, c])
        y_rest(p).start()

    def after_y_down(t, on=True):
        y_down(t).wait()
        yd[t] = add_low(yd[t], cd[t, y])
        if on:
            z_down(t).start()

    def after_y_rest(p):
        y_rest(p).wait()
        yr[p] = add_low(yr[p], cr[p, :, y])
        for i in (1, 2, 3):
            z_rest(p, i).start()

    def end_down():
        total = yd[3].astype(f32)
        for t in range(3):
            z_down(t).wait()
            total = total + zd[t].astype(f32)
        down_o[...] = total

    def end_rest(q):
        held = lax.rem(q - z + 3, 4) if q < 4 else q
        total = yr[held, z].astype(f32)
        for i in (1, 2, 3):
            z_here(q, i).wait()
            total = total + zr[q, i - 1].astype(f32)
        return total

    pltpu.make_async_copy(slot("nt"), nt_o, out_sem.at[2]).wait()
    load("wo").wait()
    for part, span in enumerate(spans):
        middle = wide[0, span, :] + dot(
            pool[SLOT["att"], :, thirds[part]], pool[SLOT["wo"]], "tn"
        )
        wide[0, span, :] = middle
        wide[2, span, :] = middle + down_bias[...]
        plain, inverse = plain_norm(middle)
        pool[SLOT["n2"], span, :] = (plain * gains[1:2, :] + shifts[1:2, :]).astype(bf16)
        low = wide[1, span, :].astype(bf16)
        pool[SLOT["g2"], span, :] = low
        sums_o[4:5, :] += jnp.sum(low.astype(f32), axis=0, keepdims=True)
    wide[3] = jnp.zeros((slots, width), f32)

    def feed(t, carry):
        two = lax.rem(t, 2)
        at = chunk_of(t)
        for copy in chunk_loads(t):
            copy.wait()

        @pl.when(t < 3)
        def _():
            for copy in chunk_loads(t + 1):
                copy.start()

        w_u = pool.at[SLOT["wu0"] + two]
        w_d = pool.at[SLOT["wd0"] + two]
        for cols in thirds:
            pre = dot(pool[SLOT["n2"]], w_u[:, cols]) + up_bias[at, :, cols]
            grad_act = dot(pool[SLOT["g2"]], w_d[cols, :], "nt")
            square = pre * pre
            gate = jnp.tanh(pre * (GELU_IN + (GELU_IN * GELU_CUBE) * square))
            gate_half = 0.5 + 0.5 * gate
            pool[SLOT["act"], :, cols] = (pre * gate_half).astype(bf16)
            slope = pre * (GELU_IN + (3.0 * GELU_IN * GELU_CUBE) * square)
            grad_pre = (grad_act * (gate_half * (1.0 + (1.0 - gate) * slope))).astype(bf16)
            pool[SLOT["gp"], :, cols] = grad_pre
            sums_o[pl.ds(5 + at, 1), cols] = jnp.sum(grad_pre.astype(f32), axis=0, keepdims=True)
        pool[SLOT["sd0"] + two] = dot(pool[SLOT["act"]], pool[SLOT["g2"]], "tn").astype(bf16)
        core_down(t).start()

        @pl.when(t > 0)
        def _():
            after_core_rest(t - 1, SLOT["sr0"] + 1 - two)

        pool[SLOT["sr0"] + two] = dot(pool[SLOT["n2"]], pool[SLOT["gp"]], "tn").astype(bf16)
        core_rest(t, SLOT["sr0"] + two).start()

        @pl.when(t == 3)
        def _():
            after_y_rest(0)

        wide[2] = wide[2] + dot(pool[SLOT["act"]], w_d[...])
        after_core_down(t)
        wide[3] = wide[3] + dot(pool[SLOT["gp"]], w_u[...], "nt")

        @pl.when(t > 1)
        def _():
            after_y_down(t - 2, True)

        return carry

    lax.fori_loop(0, 4, feed, 0)
    after_core_rest(3, SLOT["sr1"])

    pltpu.make_async_copy(wide.at[2], block_o, out_sem.at[0]).start()
    for span in spans:
        plain, inverse = plain_norm(wide[0, span, :])
        grad_two = wide[3, span, :]
        sums_o[1:2, :] += jnp.sum(grad_two * plain, axis=0, keepdims=True)
        sums_o[3:4, :] += jnp.sum(grad_two, axis=0, keepdims=True)
        middle = wide[1, span, :] + norm_backward(grad_two, plain, inverse, gains[1:2, :])
        wide[0, span, :] = middle
        pool[SLOT["gm"], span, :] = middle.astype(bf16)
    load("x_again").start()
    load("wq_again").start()
    load("nt_again").start()
    pool[SLOT["go"]] = (dot(pool[SLOT["wo"]], pool[SLOT["gm"]], "nt") * valid_row).astype(bf16)
    group = 4 * size
    for i in range(heads // 4):
        rows = slice(i * group, (i + 1) * group)
        both = pool[SLOT["att"], rows, :].astype(f32) * pool[SLOT["go"], rows, :].astype(f32)
        delta[4 * i : 4 * i + 4] = jnp.sum(both.reshape(4, size, slots), axis=1, keepdims=True)
    pool[SLOT["so"]] = dot(pool[SLOT["att"]], pool[SLOT["gm"]]).astype(bf16)
    core_rest(4, SLOT["so"]).start()
    after_core_rest(4, SLOT["so"])
    after_y_rest(1)

    def table_rows(head, found):
        for axis in range(2):
            here = found[axis * GRID : (axis + 1) * GRID]
            for bucket in range(buckets):
                kept = jnp.where(offsets[axis] == bucket, here, 0.0)
                cells[pl.ds((axis * buckets + bucket) * 16 + head, 1), :] = jnp.sum(
                    kept, axis=0, keepdims=True
                )

    def text_backward(head, carry):
        rows = rows_of(head)
        keys = by_page("k_t", rows)
        queries = masked("q_t", rows)
        grads = stack(masked("go", rows))
        scores = dot(stack(keys + [spot_twice]), stack(queries + [bias[head]]), "tn")
        prob = jnp.exp2(scores - lse[head])
        grad_prob = dot(stack(by_page("v_t", rows)), grads, "tn")
        grad_score = (prob * (grad_prob - delta[head])).astype(bf16)
        found = dot(grads, prob.astype(bf16), "nt")
        for p, cols in enumerate(thirds):
            pool[SLOT["dv"], rows, cols] = found[p * size : (p + 1) * size].astype(bf16)
        found = dot(stack(queries), grad_score, "nt") * LN2
        for p, cols in enumerate(thirds):
            pool[SLOT["dk"], rows, cols] = found[p * size : (p + 1) * size].astype(bf16)
        found = dot(stack(keys + [spot_once]), grad_score)
        pool[SLOT["dq"], rows, :] = (fold(found) * size**-0.5).astype(bf16)
        table_rows(head, found[PAGES * size :])
        return carry

    def vision_backward(head, carry):
        rows = rows_of(head)
        keys = masked("k_t", rows)
        queries = by_page("q_t", rows)
        grads = stack(by_page("go", rows))
        scores = dot(stack(keys + [bias[head]]), stack(queries + [spot_twice]), "tn")
        prob = jnp.exp2(scores - spread([lse[head, :, cols] for cols in thirds]))
        grad_prob = dot(stack(masked("v_t", rows)), grads, "tn")
        inner = spread([delta[head, :, cols] for cols in thirds])
        grad_score = (prob * (grad_prob - inner)).astype(bf16)
        pool[SLOT["dv"], rows, :] = fold(dot(grads, prob.astype(bf16), "nt")).astype(bf16)
        found = dot(stack(queries + [spot_once]), grad_score, "nt")
        pool[SLOT["dk"], rows, :] = (fold(found) * LN2).astype(bf16)
        table_rows(head, found[PAGES * size :])
        found = dot(stack(keys), grad_score) * size**-0.5
        for p, cols in enumerate(thirds):
            pool[SLOT["dq"], rows, cols] = found[p * size : (p + 1) * size].astype(bf16)
        return carry

    cells[...] = jnp.zeros_like(cells)

    @pl.when(st == 0)
    def _():
        in_pairs(text_backward)

    @pl.when(st == 1)
    def _():
        in_pairs(vision_backward)

    after_y_down(2)
    after_y_rest(2)

    def back_rows(part):
        return remote(
            slot("send").at[:, thirds[part]],
            slot("back").at[:, thirds[part]],
            xsem.at[3 + part],
            xrem.at[3 + part],
            x_peer,
        )

    for part, cols in enumerate(thirds):
        pool[SLOT["send"], :, cols] = (
            dot(pool[SLOT["wk"]], pool[SLOT["dk"], :, cols])
            + dot(pool[SLOT["wv"]], pool[SLOT["dv"], :, cols])
        ).astype(bf16)
        back_rows(part).start()
    after_y_down(3, False)
    pool[SLOT["sk"]] = dot(pool[SLOT["ft"]], pool[SLOT["dk"]], "nt").astype(bf16)
    core_rest(5, SLOT["sk"]).start()
    pool[SLOT["sv"]] = dot(pool[SLOT["ft"]], pool[SLOT["dv"]], "nt").astype(bf16)
    core_rest(6, SLOT["sv"]).start()
    after_core_rest(5, SLOT["sk"])
    load("nt_again").wait()
    pool[SLOT["sq"]] = dot(pool[SLOT["nt_again"]], pool[SLOT["dq"]], "nt").astype(bf16)
    core_rest(7, SLOT["sq"]).start()
    after_core_rest(6, SLOT["sv"])
    load("wq_again").wait()
    wide[1] = dot(pool[SLOT["wq_again"]], pool[SLOT["dq"]])
    after_core_rest(7, SLOT["sq"])

    load("x_again").wait()
    base = 2 * buckets * 16
    cells[base + 2 : base + 3, :] = valid_row
    for span in spans:
        block = wide[2, span, :]
        own = jnp.maximum(side, jnp.where(page_col[span, 0:1] < PAGES - 0.5, 1.0, 0.0))
        sub = block - wide[3, span, :]
        cells[base : base + 1, :] += jnp.sum(own * block * block, axis=0, keepdims=True)
        cells[base + 1 : base + 2, :] += jnp.sum(own * sub * sub, axis=0, keepdims=True)
    table_o[...] = lax.dot_general(
        jnp.ones((8, width), f32),
        cells[...],
        (((1,), (1,)), ((), ())),
        preferred_element_type=f32,
        precision=lax.Precision.HIGHEST,
    )

    def exchange(mine, found, send, recv, peers, at, start):
        for k in (1, 2, 3):
            copy = remote(mine, found.at[at[0]], send.at[k - 1], recv.at[k - 1], peers[k])
            if start:
                copy.start()
            else:
                copy.wait_send()
                there = lax.rem(at[0] + 4 - k, 4)
                remote(mine, found.at[there], send.at[k - 1], recv.at[k - 1], peers[k]).wait_recv()
        if not start:
            found[at[0]] = mine[...]
            mine[...] = ((found[0] + found[1]) + found[2]) + found[3]

    def small(stage, start):
        peers, at = ((place_peers, place_at), (z_peers, z_at))[stage]
        exchange(sums_o, sums_in.at[stage], asem.at[stage], arem.at[stage], peers, at, start)
        exchange(table_o, table_in.at[stage], bsem.at[stage], brem.at[stage], peers, at, start)

    def last_small(stage, start):
        peers, at = ((place_peers, place_at), (z_peers, z_at))[stage]
        exchange(late_o, late_in.at[stage], lsem.at[stage], lrem.at[stage], peers, at, start)

    def hop_copy(i):
        return remote(hop.at[i], hop_in.at[i], hsem.at[i], hrem.at[i], x_peer)

    small(0, True)
    after_y_rest(3)
    small(0, False)
    small(1, True)
    end_down()
    for q in range(4):
        up_o[:, q * width : (q + 1) * width] = end_rest(q)
    after_y_rest(4)
    small(1, False)
    table_swap = remote(table_o, table_far, fsem, frem, x_peer)
    table_swap.start()
    after_y_rest(5)
    after_y_rest(6)

    pltpu.make_async_copy(wide.at[2], block_o, out_sem.at[0]).wait()
    for part, span in enumerate(spans):
        cols = thirds[part]
        back_rows(part).wait()
        grad_one = (wide[1, :, cols] + pool[SLOT["back"], :, cols].astype(f32)).T
        plain, inverse = plain_norm(wide[3, span, :])
        late_o[0:1, :] += jnp.sum(grad_one * plain, axis=0, keepdims=True)
        late_o[1:2, :] += jnp.sum(grad_one, axis=0, keepdims=True)
        wide[2, span, :] = wide[0, span, :] + norm_backward(
            grad_one, plain, inverse, gains[0:1, :]
        )
    pltpu.make_async_copy(wide.at[2], grad_o, out_sem.at[1]).start()
    last_small(0, True)
    after_y_rest(7)
    wo_o[...] = end_rest(4)
    hop[0] = end_rest(5).astype(bf16)
    hop_copy(0).start()
    last_small(0, False)
    last_small(1, True)
    hop[1] = end_rest(6).astype(bf16)
    hop_copy(1).start()
    wq_o[...] = end_rest(7)
    table_swap.wait()
    lane = lax.broadcasted_iota(jnp.int32, table_o.shape, 1)
    table_o[...] = table_o[...] + jnp.where(lane >= base, table_far[...], 0.0)
    last_small(1, False)
    for i in range(2):
        hop_copy(i).wait()
        hop_o[i] = hop_in[i].astype(f32)
    pltpu.make_async_copy(wide.at[2], grad_o, out_sem.at[1]).wait()


def hand_over(
    block, grad_in, down, up, out, query, hop, sums, late, table,
    block_o, grad_o, gains_o, shifts_o, query_o, key_o, value_o, out_o, up_o, up_bias_o, down_o, down_bias_o, table_o, stats_o,
    held, down_h, up_h, out_h, query_h, hop_h, sums_h, late_h, table_h, in_sem, out_sem, sem,
):
    slots, width = block.shape
    step = slots // 4
    moves = []
    for i, (source, target) in enumerate(((block, block_o), (grad_in, grad_o))):
        for j in range(4):
            span = pl.ds(j * step, step)
            moves.append(
                (
                    pltpu.make_async_copy(
                        source.at[span, :], held.at[i, span, :], in_sem.at[i, j]
                    ),
                    pltpu.make_async_copy(
                        held.at[i, span, :], target.at[span, :], out_sem.at[i, j]
                    ),
                )
            )
    for move in moves:
        move[0].start()
    small = ((down, down_h), (up, up_h), (out, out_h), (query, query_h), (hop, hop_h), (sums, sums_h), (late, late_h), (table, table_h))
    small = [pltpu.make_async_copy(*pair, sem.at[i]) for i, pair in enumerate(small)]
    for copy in small:
        copy.start()
    for copy in small:
        copy.wait()
    up_o[...] = up_h[...]
    down_o[...] = down_h[...]
    gains_o[0:1, :] = late_h[0:1, :]
    gains_o[1:2, :] = sums_h[1:2, :]
    shifts_o[0:1, :] = late_h[1:2, :]
    shifts_o[1:2, :] = sums_h[3:4, :]
    down_bias_o[...] = sums_h[4:5, :]
    for q in range(4):
        up_bias_o[:, q * width : (q + 1) * width] = sums_h[5 + q : 6 + q, :]
    query_o[...] = query_h[...]
    key_o[...] = hop_h[0]
    value_o[...] = hop_h[1]
    out_o[...] = out_h[...]
    rows, heads = table_o.shape
    for row in range(rows):
        table_o[row : row + 1, :] = table_h[0:1, row * 16 : row * 16 + heads]
    total = table_h[0:1, rows * 16 : rows * 16 + 2]
    count = table_h[0:1, rows * 16 + 2 : rows * 16 + 3]
    stats_o[...] = jnp.sqrt(total / (count * width))
    for move in moves:
        move[0].wait()
        move[1].start()
    for move in moves:
        move[1].wait()


def on_device(
    inputs,
    text_pages,
    text_boxes,
    norm_gains,
    norm_shifts,
    w_query,
    w_key,
    w_value,
    w_out,
    w_up,
    up_bias,
    w_down,
    down_bias,
    box_table,
    cotangent,
):
    slots, width = inputs.shape[2:]
    rel_rows, heads = box_table.shape[1:]
    size = width // heads
    part = width // 16
    shape = lambda *dims: jax.ShapeDtypeStruct(dims, f32)
    vmem = pl.BlockSpec(memory_space=pltpu.VMEM)
    smem = pl.BlockSpec(memory_space=pltpu.SMEM)
    hbm = pl.BlockSpec(memory_space=pl.ANY)
    dma = pltpu.SemaphoreType.DMA
    cell_rows = rel_rows * 16 + 16
    low = lambda *dims: pltpu.VMEM(dims, bf16)
    full = lambda *dims: pltpu.VMEM(dims, f32)
    block, grad_in, _, down, up, out, query, hop, sums, late, table = pl.pallas_call(
        layer_kernel,
        out_shape=[
            shape(slots, width),
            shape(slots, width),
            jax.ShapeDtypeStruct((width, slots), bf16),
            shape(4 * part, width),
            shape(part, 4 * width),
            shape(part, width),
            shape(part, width),
            shape(2, part, width),
            shape(16, width),
            shape(8, width),
            shape(8, cell_rows),
        ],
        in_specs=[hbm] * 8 + [vmem] * 6 + [smem],
        out_specs=[hbm] * 3 + [vmem] * 8,
        scratch_shapes=[
            low(len(NAMES), slots, width),
            full(4, slots, width),
            low(heads, 4 * GRID, slots),
            full(heads, 1, slots),
            full(heads, 1, slots),
            low(PAGES, size, slots),
            full(slots, 128),
            full(cell_rows, width),
            low(4, 2, 4 * part, width),
            low(8, 4, 2, part, width),
            low(4, 4 * part, width),
            low(8, 4, part, width),
            low(3, 4 * part, width),
            low(8, 3, part, width),
            low(2, part, width),
            low(2, part, width),
            full(2, 4, 16, width),
            full(2, 4, 8, width),
            full(2, 4, 8, cell_rows),
            full(8, cell_rows),
            dma((7,)),
            dma((2, 2)),
            dma((3,)),
            dma((12,)),
            dma((12,)),
            dma((12,)),
            dma((12,)),
            dma((9, 3)),
            dma((9, 3)),
            dma((6,)),
            dma((6,)),
            dma((2,)),
            dma((2,)),
            dma((2, 3)),
            dma((2, 3)),
            dma((2, 3)),
            dma((2, 3)),
            dma((2, 3)),
            dma((2, 3)),
            dma,
            dma,
            dma((2,)),
            dma((2,)),
            dma((2, 3)),
            dma((2, 3)),
            dma((2,)),
            dma((2,)),
            dma((2,)),
            dma((2,)),
        ],
        compiler_params=pltpu.CompilerParams(
            collective_id=0, has_side_effects=True, vmem_limit_bytes=61 * 2**20
        ),
        name="layer",
    )(
        inputs[0, 0],
        cotangent[0, 0],
        w_query[0],
        w_key[0],
        w_value[0],
        w_out[0],
        w_up[0],
        w_down[0],
        up_bias.reshape(4, 1, width),
        down_bias,
        norm_gains[0],
        norm_shifts[0],
        text_pages,
        text_boxes[0],
        box_table[0],
    )
    outs = pl.pallas_call(
        hand_over,
        out_shape=[
            shape(slots, width),
            shape(slots, width),
            shape(2, width),
            shape(2, width),
            shape(part, width),
            shape(part, width),
            shape(part, width),
            shape(part, width),
            shape(part, 4 * width),
            shape(1, 4 * width),
            shape(4 * part, width),
            shape(1, width),
            shape(rel_rows, heads),
            shape(1, 2),
        ],
        in_specs=[hbm] * 10,
        out_specs=[hbm] * 2 + [vmem] * 12,
        scratch_shapes=[
            full(2, slots, width),
            full(4 * part, width),
            full(part, 4 * width),
            full(part, width),
            full(part, width),
            full(2, part, width),
            full(16, width),
            full(8, width),
            full(8, cell_rows),
            dma((2, 4)),
            dma((2, 4)),
            dma((8,)),
        ],
        compiler_params=pltpu.CompilerParams(vmem_limit_bytes=61 * 2**20),
        name="hand_over",
    )(block, grad_in, down, up, out, query, hop, sums, late, table)
    block, grad_in, gains, shifts, query, key, value, out, up, up_b, down, down_b, table, stats = outs
    return (
        block[None, None],
        grad_in[None, None],
        gains[None],
        shifts[None],
        query[None],
        key[None],
        value[None],
        out[None],
        up[None],
        up_b,
        down[None],
        down_b,
        table[None],
        stats[0],
    )


def partner(block, axis, bit):
    count = lax.axis_size(axis)
    route = []
    for low in range(count):
        high = low | 1 << bit
        if high != low and high < count:
            route += [(low, high), (high, low)]
    return lax.ppermute(block, axis, route)


def norm_forward(values, gain_row, shift_row):
    center = values - jnp.mean(values, axis=-1, keepdims=True)
    inverse = lax.rsqrt(jnp.mean(center * center, axis=-1, keepdims=True) + 1e-05)
    normal_part = center * inverse
    return (normal_part * gain_row + shift_row, normal_part, inverse)


def general_norm_backward(grad_normed, normal_part, inverse, gain_row):
    scaled = grad_normed * gain_row
    first_mean = jnp.mean(scaled, axis=-1, keepdims=True)
    second_mean = jnp.mean(scaled * normal_part, axis=-1, keepdims=True)
    return inverse * (scaled - first_mean - normal_part * second_mean)


def bucket_offset(own_coord, far_coord, bucket_count):
    radius = (bucket_count - 1) // 2
    return jnp.clip(own_coord[:, None] - far_coord[None, :], -radius, radius) + radius


def bias_from(rel_table, offset):
    result = jnp.zeros((rel_table.shape[1],) + offset.shape, f32)
    for bucket in range(rel_table.shape[0]):
        result = (
            result + rel_table[bucket][:, None, None] * (offset == bucket).astype(f32)[None]
        )
    return result


def bias_grad(grad_wide, offset, bucket_count):
    return jnp.stack(
        [
            jnp.sum(grad_wide * (offset == bucket).astype(f32)[None], axis=(1, 2))
            for bucket in range(bucket_count)
        ]
    )


def project(left, right):
    return jnp.einsum("rsd,de->rse", left, right, preferred_element_type=f32)


def weight_grad(left, right):
    return jnp.einsum("rsd,rse->de", left, right, preferred_element_type=f32)


def back_project(grad_low, weight):
    return jnp.einsum("rse,de->rsd", grad_low, weight, preferred_element_type=f32)


def general_device(
    inputs,
    text_pages,
    text_boxes,
    norm_gains,
    norm_shifts,
    w_query,
    w_key,
    w_value,
    w_out,
    w_up,
    up_bias,
    w_down,
    down_bias,
    box_table,
    cotangent,
):
    slot_count = inputs.shape[2]
    model_width = inputs.shape[3]
    head_count = box_table.shape[2]
    head_size = model_width // head_count
    bucket_count = box_table.shape[1] // 2
    score_scale = head_size ** (-0.5)
    is_text = lax.axis_index("stream") == 0
    positions = jnp.arange(slot_count, dtype=jnp.int32)
    cell_index = positions % (GRID * GRID)
    vision_page = positions // (GRID * GRID)
    vision_first = cell_index % GRID
    vision_second = cell_index // GRID
    own_valid = jnp.where(is_text, text_pages < PAGES, True).astype(f32)
    gain_rows = norm_gains[0]
    shift_rows = norm_shifts[0]
    rel_table = box_table[0]
    block_in = inputs[:, 0]
    normed_one, plain_one, inverse_one = norm_forward(block_in, gain_rows[0], shift_rows[0])
    normed_low = normed_one.astype(bf16)
    query = project(normed_low, w_query[0]).astype(bf16)
    own_keys = project(normed_low, w_key[0]).astype(bf16)
    own_values = project(normed_low, w_value[0]).astype(bf16)
    far_keys, far_values = partner((own_keys, own_values), "stream", 0)

    def geometry(row_index):
        text_page = text_pages[row_index]
        own_page = jnp.where(is_text, text_page, vision_page)
        far_page = jnp.where(is_text, vision_page, text_page)
        own_first = jnp.where(is_text, text_boxes[row_index, 0], vision_first)
        far_first = jnp.where(is_text, vision_first, text_boxes[row_index, 0])
        own_second = jnp.where(is_text, text_boxes[row_index, 1], vision_second)
        far_second = jnp.where(is_text, vision_second, text_boxes[row_index, 1])
        allowed = (own_page[:, None] == far_page[None, :]) | (own_page[:, None] == PAGES)
        return (
            allowed,
            bucket_offset(own_first, far_first, bucket_count),
            bucket_offset(own_second, far_second, bucket_count),
        )

    def heads_of(matrix):
        return matrix.reshape(slot_count, head_count, head_size)

    def score_block(row_index, allowed, offset_first, offset_second):
        raw = (
            jnp.einsum(
                "ihd,jhd->hij",
                heads_of(query[row_index]),
                heads_of(far_keys[row_index]),
                preferred_element_type=f32,
            )
            * score_scale
        )
        raw = (
            raw
            + bias_from(rel_table[:bucket_count], offset_first)
            + bias_from(rel_table[bucket_count:], offset_second)
        )
        return jnp.where(allowed[None], raw, masked_fill)

    row_index = 0
    allowed, offset_first, offset_second = geometry(row_index)
    masked = score_block(row_index, allowed, offset_first, offset_second)
    top_score = jnp.max(masked, axis=-1, keepdims=True)
    exp_scores = jnp.exp(masked - top_score)
    row_total = jnp.sum(exp_scores, axis=-1, keepdims=True)
    prob_low = (exp_scores / row_total).astype(bf16)
    attended = jnp.einsum(
        "hij,jhd->ihd",
        prob_low,
        heads_of(far_values[row_index]),
        preferred_element_type=f32,
    ).reshape(slot_count, model_width)
    attended_rows = [(attended * own_valid[row_index][:, None]).astype(bf16)]
    log_totals = [top_score + jnp.log(row_total)]
    attended_low = jnp.stack(attended_rows)
    branch_one = project(attended_low, w_out[0])
    middle = block_in + branch_one
    normed_two, plain_two, inverse_two = norm_forward(middle, gain_rows[1], shift_rows[1])
    normed_two_low = normed_two.astype(bf16)
    pre_act = project(normed_two_low, w_up[0]) + up_bias[0]
    act_low = jax.nn.gelu(pre_act).astype(bf16)
    branch_two = project(act_low, w_down[0]) + down_bias[0]
    block_out = middle + branch_two
    sublayer = branch_one + branch_two
    totals = lax.psum(
        (
            jnp.sum(own_valid * jnp.sum(block_out * block_out, axis=-1)),
            jnp.sum(own_valid * jnp.sum(sublayer * sublayer, axis=-1)),
            jnp.sum(own_valid),
        ),
        ("stream", "batch"),
    )
    denominator = totals[2] * model_width
    stats = jnp.stack([jnp.sqrt(totals[0] / denominator), jnp.sqrt(totals[1] / denominator)])
    grad_out = cotangent[:, 0]
    grad_out_low = grad_out.astype(bf16)
    grad_w_down = weight_grad(act_low, grad_out_low)
    grad_down_bias = jnp.sum(grad_out_low.astype(f32), axis=(0, 1))
    grad_act = back_project(grad_out_low, w_down[0])
    gelu_back = jax.vjp(jax.nn.gelu, pre_act)[1]
    grad_pre_low = gelu_back(grad_act)[0].astype(bf16)
    grad_w_up = weight_grad(normed_two_low, grad_pre_low)
    grad_up_bias = jnp.sum(grad_pre_low.astype(f32), axis=(0, 1))
    grad_normed_two = back_project(grad_pre_low, w_up[0])
    grad_gain_two = jnp.sum(grad_normed_two * plain_two, axis=(0, 1))
    grad_shift_two = jnp.sum(grad_normed_two, axis=(0, 1))
    grad_middle = grad_out + general_norm_backward(grad_normed_two, plain_two, inverse_two, gain_rows[1])
    grad_middle_low = grad_middle.astype(bf16)
    grad_w_out = weight_grad(attended_low, grad_middle_low)
    grad_attended = back_project(grad_middle_low, w_out[0]).astype(bf16) * own_valid[
        :, :, None
    ].astype(bf16)
    query_grad_rows, key_grad_rows, value_grad_rows = ([], [], [])
    row_index = 0
    allowed, offset_first, offset_second = geometry(row_index)
    masked = score_block(row_index, allowed, offset_first, offset_second)
    prob = jnp.exp(masked - log_totals[row_index])
    grad_heads = heads_of(grad_attended[row_index])
    grad_prob = jnp.einsum(
        "ihd,jhd->hij",
        grad_heads,
        heads_of(far_values[row_index]),
        preferred_element_type=f32,
    )
    inner_sum = jnp.sum(prob * grad_prob, axis=-1, keepdims=True)
    grad_score_low = (prob * (grad_prob - inner_sum)).astype(bf16)
    grad_score_wide = grad_score_low.astype(f32)
    grad_table = jnp.concatenate(
        [
            bias_grad(grad_score_wide, offset_first, bucket_count),
            bias_grad(grad_score_wide, offset_second, bucket_count),
        ],
        axis=0,
    )
    query_grad = (
        jnp.einsum(
            "hij,jhd->ihd",
            grad_score_low,
            heads_of(far_keys[row_index]),
            preferred_element_type=f32,
        )
        * score_scale
    )
    key_grad = (
        jnp.einsum(
            "hij,ihd->jhd",
            grad_score_low,
            heads_of(query[row_index]),
            preferred_element_type=f32,
        )
        * score_scale
    )
    value_grad = jnp.einsum(
        "hij,ihd->jhd", prob.astype(bf16), grad_heads, preferred_element_type=f32
    )
    query_grad_rows.append(query_grad.reshape(slot_count, model_width).astype(bf16))
    key_grad_rows.append(key_grad.reshape(slot_count, model_width).astype(bf16))
    value_grad_rows.append(value_grad.reshape(slot_count, model_width).astype(bf16))
    grad_query_low = jnp.stack(query_grad_rows)
    own_key_grad, own_value_grad = partner(
        (jnp.stack(key_grad_rows), jnp.stack(value_grad_rows)), "stream", 0
    )
    grad_w_query = weight_grad(normed_low, grad_query_low)
    grad_w_key = weight_grad(normed_low, own_key_grad)
    grad_w_value = weight_grad(normed_low, own_value_grad)
    grad_normed_one = (
        back_project(grad_query_low, w_query[0])
        + back_project(own_key_grad, w_key[0])
        + back_project(own_value_grad, w_value[0])
    )
    grad_gain_one = jnp.sum(grad_normed_one * plain_one, axis=(0, 1))
    grad_shift_one = jnp.sum(grad_normed_one, axis=(0, 1))
    grad_inputs = grad_middle + general_norm_backward(grad_normed_one, plain_one, inverse_one, gain_rows[0])
    big_sums = (
        lax.psum_scatter(grad_w_query, "batch", scatter_dimension=0, tiled=True),
        lax.psum_scatter(grad_w_key, "batch", scatter_dimension=0, tiled=True),
        lax.psum_scatter(grad_w_value, "batch", scatter_dimension=0, tiled=True),
        lax.psum_scatter(grad_w_out, "batch", scatter_dimension=0, tiled=True),
        lax.psum_scatter(grad_w_up, "batch", scatter_dimension=0, tiled=True),
        lax.psum_scatter(grad_w_down, "batch", scatter_dimension=0, tiled=True),
    )
    small_sums = lax.psum(
        (
            jnp.stack([grad_gain_one, grad_gain_two]),
            jnp.stack([grad_shift_one, grad_shift_two]),
            grad_up_bias,
            grad_down_bias,
            grad_table,
        ),
        "batch",
    )
    return (
        block_out[:, None],
        grad_inputs[:, None],
        small_sums[0][None],
        small_sums[1][None],
        big_sums[0][None],
        big_sums[1][None],
        big_sums[2][None],
        big_sums[3][None],
        big_sums[4][None],
        small_sums[2][None],
        big_sums[5][None],
        small_sums[3][None],
        small_sums[4][None],
        stats,
    )


def solution(mesh):
    sided = lambda dims: P("stream", *([None] * (dims - 1)))
    rows = P("batch", "stream", None, None)
    shard = P("stream", "batch", None)
    placed = (
        (rows, P("batch", None), P("batch", None, None), sided(3), sided(3))
        + (sided(3),) * 5
        + (sided(2), sided(3), sided(2), sided(3), rows)
    )
    fits = mesh.shape["batch"] == 16 and mesh.shape["stream"] == 2
    return jax.shard_map(
        on_device if fits else general_device,
        mesh=mesh,
        in_specs=placed,
        out_specs=(
            (rows, rows, sided(3), sided(3))
            + (shard,) * 5
            + (sided(2), shard, sided(2), sided(3), P())
        ),
        check_vma=False,
    )
```

time: 721 us -> 182 us (0.25)
  waiting for transfers between devices: 268 us -> 0 us
  matrix products: 204 us -> 0 us
  Pallas kernels: 0 us -> 178 us
  blocking collectives: 100 us -> 0 us
  other arithmetic: 89.7 us -> 0 us
  local copies, waits for them, and re-layouts: 31.1 us -> 2.74 us
  between operations: 17.1 us -> 0.66 us
    dot_general x24 -> x0, matrix products: 204 us -> none  [the longest x1 44.4 us: score_block(): jnp.einsum('ihd,jhd->hij', heads_of(query[row_index]), heads_of(far_keys[...]
    reduce_scatter x6 -> x0, waiting for transfers between devices: 200 us -> none  [the longest x1 116 us: on_device(): lax.psum_scatter(grad_w_up, 'batch', scatter_dimension=0, tiled=True)]
    pallas_call x0 -> x2, Pallas kernels: none -> 178 us  [the longest x1 171 us: on_device(): pl.pallas_call(layer_kernel, out_shape=[shape(slots, width), shape(slots,...]
    psum x2 -> x0, blocking collectives: 100 us -> none  [the longest x1 59.6 us: on_device(): lax.psum((jnp.stack([grad_gain_one, grad_gain_two]), jnp.stack([grad_shif...]
    ppermute x4 -> x0, waiting for transfers between devices: 68 us -> none  [partner(): return lax.ppermute(block, axis, route)]
    reduce_sum x7 -> x0, other arithmetic: 64.4 us -> none  [the longest x1 48 us: bias_grad(): jnp.sum(grad_wide * (offset == bucket).astype(jnp.float32)[None], axis=(1...]
    unnamed x141 -> x2, local copies, waits for them, and re-layouts: 19.6 us -> 2.74 us
    convert_element_type x5 -> x0, other arithmetic: 16 us -> none  [the longest x2 13.7 us: bias_from(): (offset == bucket).astype(jnp.float32)[None]]
  transfers between devices with their start and end apart: 10 -> 0, of which waited for: 5 -> 0; matrix products, arithmetic and copies ran while one was open for 34% -> 0% of each run, Pallas kernels for 0% -> 0%
where the time goes in v3:
time: 182 us; the launch traced here: 181 us
  Pallas kernels  178 us (98%)
  local copies, waits for them, and re-layouts  2.74 us (2%)
    pallas_call x1, Pallas kernels, on_device(): pl.pallas_call(layer_kernel, out_shape=[shape(slots, width), shape(slots,...  171 us
    pallas_call x1, Pallas kernels, on_device(): pl.pallas_call(hand_over, out_shape=[shape(slots, width), shape(slots, wi...  6.55 us

profile of v3, /device:TPU:0, one launch (start us, length us, event | category | flops | bytes accessed | tf_op | source)
XLA Modules:
  0.0 181.3 jit_solution(6938297482533103476)
XLA Ops:
  0.6 1.4 copy.29
  2.0 171.3 %layer.1 = (f32[768,768]{1,0:T(8,128)}, f32[768,768]{1,0:T(8,128)}, bf16[768,768]{1,0:T(8,128)(2,1)}, f32[192,768]{1,0:T(8,128)}, f32[48,3072]{1,0:T(8,128)}, /*...) custom-call(f32[768,768]{1,0:T(8,128)} %bitcast.27, ...), custom_call_target="tpu_custom_call" | custom-call | tf_op jit(solution)/shard_map/layer/pallas_call | solution.py:756
  173.3 6.5 %hand_over.1 = (f32[768,768]{1,0:T(8,128)}, f32[768,768]{1,0:T(8,128)}, f32[2,768]{1,0:T(2,128)}, f32[2,768]{1,0:T(2,128)}, f32[48,768]{1,0:T(8,128)}, /*index=5...) custom-call(f32[768,768]{1,0:T(8,128)} %get-tuple-element.38.block, ...), custom_call_target="tpu_custom_call" | custom-call | tf_op jit(solution)/shard_map/hand_over/pallas_call | solution.py:845
  179.9 1.4 copy.30
